TPU v7x, 32 devices: a whole 2x2x4 slice. The times are simulated.
32 devices in a mesh: seq: 16 (over z, y, x), dp: 2 (over core).
Axes of the slice: x: 2, y: 2, z: 4, core: 2. Of those that a mesh axis runs over, the one named last changes fastest.
Arguments:
- tokens: bfloat16 [2, 12288, 768], P('dp', 'seq'), may hold values from -6 to 6
- lengths: int32 [2, 3], P('dp'), may hold values from 2049 to 4096, as said below
- cotangent: bfloat16 [2, 12288, 768], P('dp', 'seq'), may hold values from -6 to 6
- norm1_gain: float32 [768], replicated, may hold values from 0.25 to 1.75
- norm1_shift: float32 [768], replicated, may hold values from -3 to 3
- query_weight: bfloat16 [768, 768], replicated, may hold values from -0.21875 to 0.21875
- query_bias: float32 [768], replicated, may hold values from -3 to 3
- keyval_weight: bfloat16 [768, 128], replicated, may hold values from -0.21875 to 0.21875
- value_bias: float32 [64], replicated, may hold values from -3 to 3
- out_weight: bfloat16 [768, 768], replicated, may hold values from -6 to 6
- out_bias: float32 [768], replicated, may hold values from -3 to 3
- norm2_gain: float32 [768], replicated, may hold values from 0.25 to 1.75
- norm2_shift: float32 [768], replicated, may hold values from -3 to 3
- up_weight: bfloat16 [768, 3072], replicated, may hold values from -0.21875 to 0.21875
- up_bias: float32 [3072], replicated, may hold values from -3 to 3
- down_weight: bfloat16 [3072, 768], replicated, may hold values from -0.109375 to 0.109375
- down_bias: float32 [768], replicated, may hold values from -3 to 3
Outputs:
- out_tokens: bfloat16 [2, 12288, 768], P('dp', 'seq')
- grad_tokens: float32 [2, 12288, 768], P('dp', 'seq')
- grad_norm1_gain: float32 [768], replicated
- grad_norm1_shift: float32 [768], replicated
- grad_query_weight: float32 [768, 768], replicated
- grad_query_bias: float32 [768], replicated
- grad_keyval_weight: float32 [768, 128], replicated
- grad_value_bias: float32 [64], replicated
- grad_out_weight: float32 [768, 768], replicated
- grad_out_bias: float32 [768], replicated
- grad_norm2_gain: float32 [768], replicated
- grad_norm2_shift: float32 [768], replicated
- grad_up_weight: float32 [768, 3072], replicated
- grad_up_bias: float32 [3072], replicated
- grad_down_weight: float32 [3072, 768], replicated
- grad_down_bias: float32 [768], replicated
Inputs may be any that keep to these rules, and one draw needn't show every extreme that they name: `lengths`: valid tokens of each 4096-slot row, the valid ones first; every group has at least one row with all 4096 slots valid.
All inputs are finite; a program needn't handle non-finite values.
Results may differ from a plain program's by a relative error of at most 0.011.
Values may be sent and summed in bfloat16 or wider, within the bound.
A program may use at most 320 MiB of HBM per device.

v0:
```python
from functools import partial

import jax
import jax.numpy as jnp
from jax import lax
from jax.sharding import PartitionSpec as P

ROW = 4096


epsilon = 1e-05
masked_score = -1e30


def shifted(value, axis, by):
    devices = lax.axis_size(axis)
    pairs = [(i, i + by) for i in range(devices) if 0 <= i + by < devices]
    return lax.ppermute(value, axis, pairs)


def normed(values, gains, shifts):
    center = values - jnp.mean(values, axis=-1, keepdims=True)
    spread = jnp.mean(center * center, axis=-1, keepdims=True)
    return center * lax.rsqrt(spread + epsilon) * gains + shifts


def matmul(left_op, right_op):
    return jnp.dot(left_op, right_op, preferred_element_type=jnp.float32)


def over_rows(left_op, right_op):
    return lax.dot_general(
        left_op, right_op, (((0,), (0,)), ((), ())), preferred_element_type=jnp.float32
    )


def over_cols(left_op, right_op):
    return lax.dot_general(
        left_op, right_op, (((1,), (1,)), ((), ())), preferred_element_type=jnp.float32
    )


def per_device(
    tokens,
    lengths,
    cotangent,
    norm1_gain,
    norm1_shift,
    query_weight,
    query_bias,
    keyval_weight,
    value_bias,
    out_weight,
    out_bias,
    norm2_gain,
    norm2_shift,
    up_weight,
    up_bias,
    down_weight,
    down_bias,
):
    devices = lax.axis_size("seq")
    device_id = lax.axis_index("seq")
    shard_len = tokens.shape[1]
    model_width = tokens.shape[2]
    head_dim = keyval_weight.shape[1] // 2
    heads_all = model_width // head_dim
    groups = heads_all // 2
    scaling = head_dim ** (-0.5)
    hop_count = min((ROW - 2) // shard_len + 1, devices - 1)
    row_count = lengths.shape[1]
    inputs = tokens[0].astype(jnp.float32)
    positions = device_id * shard_len + jnp.arange(shard_len, dtype=jnp.int32)
    row_index = jnp.arange(row_count, dtype=jnp.int32)
    row_lengths = lengths[0]

    def key_masks(source):
        key_pos = source * shard_len + jnp.arange(shard_len, dtype=jnp.int32)
        key_row = jnp.floor_divide(key_pos, ROW)
        row_limit = jnp.sum(
            jnp.where(key_row[:, None] == row_index[None, :], row_lengths[None, :], 0), axis=1
        )
        key_live = key_pos - key_row * ROW < row_limit
        same_row = jnp.floor_divide(positions, ROW)[:, None] == key_row[None, :]
        return same_row & (key_pos[None, :] <= positions[:, None]) & key_live[None, :]

    normal_one = normed(inputs, norm1_gain, norm1_shift).astype(jnp.bfloat16)
    queries = (matmul(normal_one, query_weight) + query_bias).astype(jnp.bfloat16)
    kv_bias = jnp.concatenate([jnp.zeros((head_dim,), jnp.float32), value_bias])
    keyvals = (matmul(normal_one, keyval_weight) + kv_bias).astype(jnp.bfloat16)
    remote = [shifted(keyvals, "seq", offset) for offset in range(1, hop_count + 1)]
    all_keys = jnp.concatenate([keyvals] + remote, axis=0)
    key_mask = jnp.concatenate(
        [key_masks(device_id - offset) for offset in range(hop_count + 1)], axis=1
    )
    key_part = all_keys[:, :head_dim]
    val_part = all_keys[:, head_dim:]
    query_groups = queries.reshape(shard_len, groups, 2, head_dim).transpose(1, 0, 2, 3)

    def scores_of(query_pair):
        raw_scores = (
            jnp.einsum("qhd,kd->hqk", query_pair, key_part, preferred_element_type=jnp.float32)
            * scaling
        )
        return jnp.where(key_mask[None], raw_scores, masked_score)

    def forward_pair(query_pair):
        scores = scores_of(query_pair)
        row_max = jnp.max(scores, axis=-1, keepdims=True)
        exponent = jnp.exp(scores - row_max)
        row_total = jnp.sum(exponent, axis=-1, keepdims=True)
        prob_low = (exponent / row_total).astype(jnp.bfloat16)
        mixture = jnp.einsum("hqk,kd->qhd", prob_low, val_part, preferred_element_type=jnp.float32)
        return (mixture, row_max + jnp.log(row_total))

    mixture, log_sums = lax.map(forward_pair, query_groups)
    attended = mixture.transpose(1, 0, 2, 3).reshape(shard_len, model_width).astype(jnp.bfloat16)
    residual = inputs + matmul(attended, out_weight) + out_bias
    normal_two = normed(residual, norm2_gain, norm2_shift).astype(jnp.bfloat16)
    hidden_pre = matmul(normal_two, up_weight) + up_bias
    activated = jax.nn.gelu(hidden_pre, approximate=True).astype(jnp.bfloat16)
    outputs = residual + matmul(activated, down_weight) + down_bias
    upstream = cotangent[0]
    upstream_wide = upstream.astype(jnp.float32)
    grad_down = over_rows(activated, upstream)
    grad_down_bias = jnp.sum(upstream_wide, axis=0)
    grad_act = over_cols(upstream, down_weight)
    _, gelu_back = jax.vjp(partial(jax.nn.gelu, approximate=True), hidden_pre)
    grad_hidden = gelu_back(grad_act)[0].astype(jnp.bfloat16)
    grad_up = over_rows(normal_two, grad_hidden)
    grad_up_bias = jnp.sum(grad_hidden.astype(jnp.float32), axis=0)
    grad_normal_two = over_cols(grad_hidden, up_weight)
    _, norm_two_back = jax.vjp(normed, residual, norm2_gain, norm2_shift)
    grad_res_part, grad_gain_two, grad_shift_two = norm_two_back(grad_normal_two)
    grad_residual = upstream_wide + grad_res_part
    grad_proj = grad_residual.astype(jnp.bfloat16)
    grad_out_w = over_rows(attended, grad_proj)
    grad_out_b = jnp.sum(grad_proj.astype(jnp.float32), axis=0)
    grad_att = over_cols(grad_proj, out_weight).astype(jnp.bfloat16)
    grad_groups = grad_att.reshape(shard_len, groups, 2, head_dim).transpose(1, 0, 2, 3)

    def backward_pair(running, pieces):
        query_pair, grad_pair, log_pair = pieces
        scores = scores_of(query_pair)
        probability = jnp.exp(scores - log_pair)
        prob_low = probability.astype(jnp.bfloat16)
        grad_probs = jnp.einsum(
            "qhd,kd->hqk", grad_pair, val_part, preferred_element_type=jnp.float32
        )
        centered = grad_probs - jnp.sum(grad_probs * probability, axis=-1, keepdims=True)
        grad_scores = (probability * centered).astype(jnp.bfloat16)
        grad_query = (
            jnp.einsum("hqk,kd->qhd", grad_scores, key_part, preferred_element_type=jnp.float32)
            * scaling
        )
        grad_keys = (
            running[0]
            + jnp.einsum("hqk,qhd->kd", grad_scores, query_pair, preferred_element_type=jnp.float32)
            * scaling
        )
        grad_vals = running[1] + jnp.einsum(
            "hqk,qhd->kd", prob_low, grad_pair, preferred_element_type=jnp.float32
        )
        return ((grad_keys, grad_vals), grad_query)

    zero_keys = jnp.zeros((all_keys.shape[0], head_dim), jnp.float32)
    (grad_keys, grad_vals), grad_query = lax.scan(
        backward_pair, (zero_keys, zero_keys), (query_groups, grad_groups, log_sums)
    )
    grad_all = jnp.concatenate([grad_keys, grad_vals], axis=1)
    blocks = [
        grad_all[offset * shard_len : (offset + 1) * shard_len] for offset in range(hop_count + 1)
    ]
    returned = blocks[0]
    for offset in range(1, hop_count + 1):
        returned = returned + shifted(blocks[offset], "seq", -offset)
    grad_kv = returned.astype(jnp.bfloat16)
    grad_queries = (
        grad_query.transpose(1, 0, 2, 3).reshape(shard_len, model_width).astype(jnp.bfloat16)
    )
    grad_qw = over_rows(normal_one, grad_queries)
    grad_qb = jnp.sum(grad_queries.astype(jnp.float32), axis=0)
    grad_kvw = over_rows(normal_one, grad_kv)
    grad_vb = jnp.sum(grad_kv[:, head_dim:].astype(jnp.float32), axis=0)
    grad_normal_one = over_cols(grad_queries, query_weight) + over_cols(grad_kv, keyval_weight)
    _, norm_one_back = jax.vjp(normed, inputs, norm1_gain, norm1_shift)
    grad_in_part, grad_gain_one, grad_shift_one = norm_one_back(grad_normal_one)
    grad_inputs = grad_residual + grad_in_part
    summed = tuple(
        lax.psum(
            (
                grad_gain_one,
                grad_shift_one,
                grad_qw,
                grad_qb,
                grad_kvw,
                grad_vb,
                grad_out_w,
                grad_out_b,
                grad_gain_two,
                grad_shift_two,
                grad_up,
                grad_up_bias,
                grad_down,
                grad_down_bias,
            ),
            ("seq", "dp"),
        )
    )
    return (outputs.astype(jnp.bfloat16)[None], grad_inputs[None]) + summed


def solution(mesh):
    placed = (
        P("dp", "seq", None),
        P("dp", None),
        P("dp", "seq", None),
        P(),
        P(),
        P(),
        P(),
        P(),
        P(),
        P(),
        P(),
        P(),
        P(),
        P(),
        P(),
        P(),
        P(),
    )
    return jax.shard_map(
        per_device,
        mesh=mesh,
        in_specs=placed,
        out_specs=(
            P("dp", "seq", None),
            P("dp", "seq", None),
            P(),
            P(),
            P(),
            P(),
            P(),
            P(),
            P(),
            P(),
            P(),
            P(),
            P(),
            P(),
            P(),
            P(),
        ),
        check_vma=False,
    )
```

profile of v0, /device:TPU:0, one launch (start us, length us, event | category | flops | bytes accessed | tf_op | source)
XLA Modules:
  0.0 1537.6 jit_solution(134189211929620216)
XLA Ops:
  64.8 290.5 %while.27 = (s32[]{:T(128)}, bf16[6,768,2,64]{1,3,2,0:T(8,128)(2,1)}, f32[6,2,768,1]{2,1,3,0:T(2,128)S(1)}, pred[768,5376]{1,0:T(8,128)(4,1)}, bf16[6,768,2,64]{...) while((s32[]{:T(128)}, ...), condition=%wide.region_12.13_spmd, body=%wide.region_9.12_spmd.sunk | while | flops 2213018112 | bytes 113492072 | solution.py:116
  79.3 16.3 %fusion.180 = f32[2,768]{1,0:T(2,128)S(1)} fusion(f32[768,2,5376]{2,0,1:T(8,128)} %get-tuple-element.412, f32[2,768]{1,0:T(2,128)S(1)} %get-tuple-element.413, pred[768,5376]{1,0:T(8,128)(4,1)} %get-tuple-element.445), kind=kLoop, calls=%fused_computation.5.clone.1 | loop fusion | flops 33028608 | bytes 37171200 | tf_op jit(solution)/shard_map/while/body/eval_jaxpr/reduce_sum | solution.py:111
  95.6 17.6 %fusion.181 = bf16[6,768,2,64]{1,3,2,0:T(8,128)(2,1)} fusion(bf16[6,768,2,64]{1,3,2,0:T(8,128)(2,1)} %get-tuple-element.435, s32[]{:T(128)S(6)} %copy.80, f32[768,2,5376]{2,0,1:T(8,128)} %get-tuple-element.412, f32[2,768]{1,0:T(2,128)S(1)} %fusion.180, f32[2,768]{1,0:T(2,128)S(1)} %get-tuple-element.413, pred[768,5376]{1,0:T(8,128)(4,1)} %get-tuple-element.445, ...), kind=kOutput, calls=%fused_computation.8.clone.1 | convolution fusion | flops 1098252288 | bytes 38252548 | tf_op jit(solution)/shard_map/while/body/eval_jaxpr/hqk,kd->qhd/dot_general | solution.py:113
  127.6 16.3 %fusion.180 = f32[2,768]{1,0:T(2,128)S(1)} fusion(f32[768,2,5376]{2,0,1:T(8,128)} %get-tuple-element.412, f32[2,768]{1,0:T(2,128)S(1)} %get-tuple-element.413, pred[768,5376]{1,0:T(8,128)(4,1)} %get-tuple-element.445), kind=kLoop, calls=%fused_computation.5.clone.1 | loop fusion | flops 33028608 | bytes 37171200 | tf_op jit(solution)/shard_map/while/body/eval_jaxpr/reduce_sum | solution.py:111
  143.9 17.6 %fusion.181 = bf16[6,768,2,64]{1,3,2,0:T(8,128)(2,1)} fusion(bf16[6,768,2,64]{1,3,2,0:T(8,128)(2,1)} %get-tuple-element.435, s32[]{:T(128)S(6)} %copy.80, f32[768,2,5376]{2,0,1:T(8,128)} %get-tuple-element.412, f32[2,768]{1,0:T(2,128)S(1)} %fusion.180, f32[2,768]{1,0:T(2,128)S(1)} %get-tuple-element.413, pred[768,5376]{1,0:T(8,128)(4,1)} %get-tuple-element.445, ...), kind=kOutput, calls=%fused_computation.8.clone.1 | convolution fusion | flops 1098252288 | bytes 38252548 | tf_op jit(solution)/shard_map/while/body/eval_jaxpr/hqk,kd->qhd/dot_general | solution.py:113
  175.9 16.3 %fusion.180 = f32[2,768]{1,0:T(2,128)S(1)} fusion(f32[768,2,5376]{2,0,1:T(8,128)} %get-tuple-element.412, f32[2,768]{1,0:T(2,128)S(1)} %get-tuple-element.413, pred[768,5376]{1,0:T(8,128)(4,1)} %get-tuple-element.445), kind=kLoop, calls=%fused_computation.5.clone.1 | loop fusion | flops 33028608 | bytes 37171200 | tf_op jit(solution)/shard_map/while/body/eval_jaxpr/reduce_sum | solution.py:111
  192.3 17.6 %fusion.181 = bf16[6,768,2,64]{1,3,2,0:T(8,128)(2,1)} fusion(bf16[6,768,2,64]{1,3,2,0:T(8,128)(2,1)} %get-tuple-element.435, s32[]{:T(128)S(6)} %copy.80, f32[768,2,5376]{2,0,1:T(8,128)} %get-tuple-element.412, f32[2,768]{1,0:T(2,128)S(1)} %fusion.180, f32[2,768]{1,0:T(2,128)S(1)} %get-tuple-element.413, pred[768,5376]{1,0:T(8,128)(4,1)} %get-tuple-element.445, ...), kind=kOutput, calls=%fused_computation.8.clone.1 | convolution fusion | flops 1098252288 | bytes 38252548 | tf_op jit(solution)/shard_map/while/body/eval_jaxpr/hqk,kd->qhd/dot_general | solution.py:113
  240.6 17.6 %fusion.181 = bf16[6,768,2,64]{1,3,2,0:T(8,128)(2,1)} fusion(bf16[6,768,2,64]{1,3,2,0:T(8,128)(2,1)} %get-tuple-element.435, s32[]{:T(128)S(6)} %copy.80, f32[768,2,5376]{2,0,1:T(8,128)} %get-tuple-element.412, f32[2,768]{1,0:T(2,128)S(1)} %fusion.180, f32[2,768]{1,0:T(2,128)S(1)} %get-tuple-element.413, pred[768,5376]{1,0:T(8,128)(4,1)} %get-tuple-element.445, ...), kind=kOutput, calls=%fused_computation.8.clone.1 | convolution fusion | flops 1098252288 | bytes 38252548 | tf_op jit(solution)/shard_map/while/body/eval_jaxpr/hqk,kd->qhd/dot_general | solution.py:113
  272.6 16.3 %fusion.180 = f32[2,768]{1,0:T(2,128)S(1)} fusion(f32[768,2,5376]{2,0,1:T(8,128)} %get-tuple-element.412, f32[2,768]{1,0:T(2,128)S(1)} %get-tuple-element.413, pred[768,5376]{1,0:T(8,128)(4,1)} %get-tuple-element.445), kind=kLoop, calls=%fused_computation.5.clone.1 | loop fusion | flops 33028608 | bytes 37171200 | tf_op jit(solution)/shard_map/while/body/eval_jaxpr/reduce_sum | solution.py:111
  288.9 17.6 %fusion.181 = bf16[6,768,2,64]{1,3,2,0:T(8,128)(2,1)} fusion(bf16[6,768,2,64]{1,3,2,0:T(8,128)(2,1)} %get-tuple-element.435, s32[]{:T(128)S(6)} %copy.80, f32[768,2,5376]{2,0,1:T(8,128)} %get-tuple-element.412, f32[2,768]{1,0:T(2,128)S(1)} %fusion.180, f32[2,768]{1,0:T(2,128)S(1)} %get-tuple-element.413, pred[768,5376]{1,0:T(8,128)(4,1)} %get-tuple-element.445, ...), kind=kOutput, calls=%fused_computation.8.clone.1 | convolution fusion | flops 1098252288 | bytes 38252548 | tf_op jit(solution)/shard_map/while/body/eval_jaxpr/hqk,kd->qhd/dot_general | solution.py:113
  337.2 17.6 %fusion.181 = bf16[6,768,2,64]{1,3,2,0:T(8,128)(2,1)} fusion(bf16[6,768,2,64]{1,3,2,0:T(8,128)(2,1)} %get-tuple-element.435, s32[]{:T(128)S(6)} %copy.80, f32[768,2,5376]{2,0,1:T(8,128)} %get-tuple-element.412, f32[2,768]{1,0:T(2,128)S(1)} %fusion.180, f32[2,768]{1,0:T(2,128)S(1)} %get-tuple-element.413, pred[768,5376]{1,0:T(8,128)(4,1)} %get-tuple-element.445, ...), kind=kOutput, calls=%fused_computation.8.clone.1 | convolution fusion | flops 1098252288 | bytes 38252548 | tf_op jit(solution)/shard_map/while/body/eval_jaxpr/hqk,kd->qhd/dot_general | solution.py:113
  403.6 651.7 %while.28 = (s32[]{:T(128)}, f32[5376,64]{0,1:T(8,128)S(1)}, f32[5376,64]{0,1:T(8,128)}, bf16[6,768,2,64]{1,3,2,0:T(8,128)(2,1)}, pred[768,5376]{1,0:T(8,128)(4,...) while((s32[]{:T(128)}, f32[5376,64]{0,1:T(8,128)S(1)}, ...), condition=%wide.region_19.20_spmd.clone, body=%wide.region_17.19_spmd.clone.sunk | while | flops 5410503168 | bytes 271657152 | solution.py:167
  417.8 27.9 %fusion.191 = (f32[2,768]{1,0:T(2,128)S(1)}, f32[768,2,5376]{2,0,1:T(8,128)}) fusion(f32[768,2,5376]{2,0,1:T(8,128)} %fusion.190, f32[2,768]{1,0:T(2,128)S(1)} %dynamic-slice_bitcast_fusion.2, pred[768,5376]{1,0:T(8,128)(4,1)} %get-tuple-element.478, bf16[5376,64]{0,1:T(8,128)(2,1)S(1)} %copy-done.9, ...), kind=kOutput, calls=%fused_computation.20.clone.1 | convolution fusion | flops 1098250752 | bytes 71086080 | tf_op jit(solution)/shard_map/while/body/eval_jaxpr/qhd,kd->hqk/dot_general | solution.py:147
  445.7 28.7 %fusion.192 = bf16[2,768,5376]{2,1,0:T(8,128)(2,1)} fusion(f32[768,2,5376]{2,0,1:T(8,128)} %get-tuple-element.424, f32[768,2,5376]{2,0,1:T(8,128)} %fusion.190, f32[2,768]{1,0:T(2,128)S(1)} %get-tuple-element.425, f32[2,768]{1,0:T(2,128)S(1)} %dynamic-slice_bitcast_fusion.2, pred[768,5376]{1,0:T(8,128)(4,1)} %get-tuple-element.478), kind=kLoop, calls=%fused_computation.22.clone.1 | loop fusion | flops 49545216 | bytes 86716416 | tf_op jit(solution)/shard_map/while/body/eval_jaxpr/convert_element_type | solution.py:151
  483.3 17.3 %fusion.194 = f32[5376,64]{0,1:T(8,128)} fusion(f32[768,2,5376]{2,0,1:T(8,128)} %fusion.190, f32[2,768]{1,0:T(2,128)S(1)} %dynamic-slice_bitcast_fusion.2, pred[768,5376]{1,0:T(8,128)(4,1)} %get-tuple-element.478, f32[5376,64]{0,1:T(8,128)} %get-tuple-element.464, pred[]{:T(512)S(6)} %compare.116, bf16[6,768,2,64]{1,3,2,0:T(8,128)(2,1)} %get-tuple-element.482, ...), kind=kOutput, calls=%fused_computation.32.clone.1 | convolution fusion | flops 1090682880 | bytes 40114180 | tf_op jit(solution)/shard_map/while/body/eval_jaxpr/hqk,qhd->kd/dot_general | solution.py:161
  526.1 27.9 %fusion.191 = (f32[2,768]{1,0:T(2,128)S(1)}, f32[768,2,5376]{2,0,1:T(8,128)}) fusion(f32[768,2,5376]{2,0,1:T(8,128)} %fusion.190, f32[2,768]{1,0:T(2,128)S(1)} %dynamic-slice_bitcast_fusion.2, pred[768,5376]{1,0:T(8,128)(4,1)} %get-tuple-element.478, bf16[5376,64]{0,1:T(8,128)(2,1)S(1)} %copy-done.9, ...), kind=kOutput, calls=%fused_computation.20.clone.1 | convolution fusion | flops 1098250752 | bytes 71086080 | tf_op jit(solution)/shard_map/while/body/eval_jaxpr/qhd,kd->hqk/dot_general | solution.py:147
  554.0 28.7 %fusion.192 = bf16[2,768,5376]{2,1,0:T(8,128)(2,1)} fusion(f32[768,2,5376]{2,0,1:T(8,128)} %get-tuple-element.424, f32[768,2,5376]{2,0,1:T(8,128)} %fusion.190, f32[2,768]{1,0:T(2,128)S(1)} %get-tuple-element.425, f32[2,768]{1,0:T(2,128)S(1)} %dynamic-slice_bitcast_fusion.2, pred[768,5376]{1,0:T(8,128)(4,1)} %get-tuple-element.478), kind=kLoop, calls=%fused_computation.22.clone.1 | loop fusion | flops 49545216 | bytes 86716416 | tf_op jit(solution)/shard_map/while/body/eval_jaxpr/convert_element_type | solution.py:151
  591.6 17.6 %fusion.194 = f32[5376,64]{0,1:T(8,128)} fusion(f32[768,2,5376]{2,0,1:T(8,128)} %fusion.190, f32[2,768]{1,0:T(2,128)S(1)} %dynamic-slice_bitcast_fusion.2, pred[768,5376]{1,0:T(8,128)(4,1)} %get-tuple-element.478, f32[5376,64]{0,1:T(8,128)} %get-tuple-element.464, pred[]{:T(512)S(6)} %compare.116, bf16[6,768,2,64]{1,3,2,0:T(8,128)(2,1)} %get-tuple-element.482, ...), kind=kOutput, calls=%fused_computation.32.clone.1 | convolution fusion | flops 1090682880 | bytes 40114180 | tf_op jit(solution)/shard_map/while/body/eval_jaxpr/hqk,qhd->kd/dot_general | solution.py:161
  634.7 27.9 %fusion.191 = (f32[2,768]{1,0:T(2,128)S(1)}, f32[768,2,5376]{2,0,1:T(8,128)}) fusion(f32[768,2,5376]{2,0,1:T(8,128)} %fusion.190, f32[2,768]{1,0:T(2,128)S(1)} %dynamic-slice_bitcast_fusion.2, pred[768,5376]{1,0:T(8,128)(4,1)} %get-tuple-element.478, bf16[5376,64]{0,1:T(8,128)(2,1)S(1)} %copy-done.9, ...), kind=kOutput, calls=%fused_computation.20.clone.1 | convolution fusion | flops 1098250752 | bytes 71086080 | tf_op jit(solution)/shard_map/while/body/eval_jaxpr/qhd,kd->hqk/dot_general | solution.py:147
  662.6 28.7 %fusion.192 = bf16[2,768,5376]{2,1,0:T(8,128)(2,1)} fusion(f32[768,2,5376]{2,0,1:T(8,128)} %get-tuple-element.424, f32[768,2,5376]{2,0,1:T(8,128)} %fusion.190, f32[2,768]{1,0:T(2,128)S(1)} %get-tuple-element.425, f32[2,768]{1,0:T(2,128)S(1)} %dynamic-slice_bitcast_fusion.2, pred[768,5376]{1,0:T(8,128)(4,1)} %get-tuple-element.478), kind=kLoop, calls=%fused_computation.22.clone.1 | loop fusion | flops 49545216 | bytes 86716416 | tf_op jit(solution)/shard_map/while/body/eval_jaxpr/convert_element_type | solution.py:151
  700.2 17.6 %fusion.194 = f32[5376,64]{0,1:T(8,128)} fusion(f32[768,2,5376]{2,0,1:T(8,128)} %fusion.190, f32[2,768]{1,0:T(2,128)S(1)} %dynamic-slice_bitcast_fusion.2, pred[768,5376]{1,0:T(8,128)(4,1)} %get-tuple-element.478, f32[5376,64]{0,1:T(8,128)} %get-tuple-element.464, pred[]{:T(512)S(6)} %compare.116, bf16[6,768,2,64]{1,3,2,0:T(8,128)(2,1)} %get-tuple-element.482, ...), kind=kOutput, calls=%fused_computation.32.clone.1 | convolution fusion | flops 1090682880 | bytes 40114180 | tf_op jit(solution)/shard_map/while/body/eval_jaxpr/hqk,qhd->kd/dot_general | solution.py:161
  743.3 27.9 %fusion.191 = (f32[2,768]{1,0:T(2,128)S(1)}, f32[768,2,5376]{2,0,1:T(8,128)}) fusion(f32[768,2,5376]{2,0,1:T(8,128)} %fusion.190, f32[2,768]{1,0:T(2,128)S(1)} %dynamic-slice_bitcast_fusion.2, pred[768,5376]{1,0:T(8,128)(4,1)} %get-tuple-element.478, bf16[5376,64]{0,1:T(8,128)(2,1)S(1)} %copy-done.9, ...), kind=kOutput, calls=%fused_computation.20.clone.1 | convolution fusion | flops 1098250752 | bytes 71086080 | tf_op jit(solution)/shard_map/while/body/eval_jaxpr/qhd,kd->hqk/dot_general | solution.py:147
  771.2 28.7 %fusion.192 = bf16[2,768,5376]{2,1,0:T(8,128)(2,1)} fusion(f32[768,2,5376]{2,0,1:T(8,128)} %get-tuple-element.424, f32[768,2,5376]{2,0,1:T(8,128)} %fusion.190, f32[2,768]{1,0:T(2,128)S(1)} %get-tuple-element.425, f32[2,768]{1,0:T(2,128)S(1)} %dynamic-slice_bitcast_fusion.2, pred[768,5376]{1,0:T(8,128)(4,1)} %get-tuple-element.478), kind=kLoop, calls=%fused_computation.22.clone.1 | loop fusion | flops 49545216 | bytes 86716416 | tf_op jit(solution)/shard_map/while/body/eval_jaxpr/convert_element_type | solution.py:151
  808.8 17.6 %fusion.194 = f32[5376,64]{0,1:T(8,128)} fusion(f32[768,2,5376]{2,0,1:T(8,128)} %fusion.190, f32[2,768]{1,0:T(2,128)S(1)} %dynamic-slice_bitcast_fusion.2, pred[768,5376]{1,0:T(8,128)(4,1)} %get-tuple-element.478, f32[5376,64]{0,1:T(8,128)} %get-tuple-element.464, pred[]{:T(512)S(6)} %compare.116, bf16[6,768,2,64]{1,3,2,0:T(8,128)(2,1)} %get-tuple-element.482, ...), kind=kOutput, calls=%fused_computation.32.clone.1 | convolution fusion | flops 1090682880 | bytes 40114180 | tf_op jit(solution)/shard_map/while/body/eval_jaxpr/hqk,qhd->kd/dot_general | solution.py:161
  851.9 27.9 %fusion.191 = (f32[2,768]{1,0:T(2,128)S(1)}, f32[768,2,5376]{2,0,1:T(8,128)}) fusion(f32[768,2,5376]{2,0,1:T(8,128)} %fusion.190, f32[2,768]{1,0:T(2,128)S(1)} %dynamic-slice_bitcast_fusion.2, pred[768,5376]{1,0:T(8,128)(4,1)} %get-tuple-element.478, bf16[5376,64]{0,1:T(8,128)(2,1)S(1)} %copy-done.9, ...), kind=kOutput, calls=%fused_computation.20.clone.1 | convolution fusion | flops 1098250752 | bytes 71086080 | tf_op jit(solution)/shard_map/while/body/eval_jaxpr/qhd,kd->hqk/dot_general | solution.py:147
  879.8 28.7 %fusion.192 = bf16[2,768,5376]{2,1,0:T(8,128)(2,1)} fusion(f32[768,2,5376]{2,0,1:T(8,128)} %get-tuple-element.424, f32[768,2,5376]{2,0,1:T(8,128)} %fusion.190, f32[2,768]{1,0:T(2,128)S(1)} %get-tuple-element.425, f32[2,768]{1,0:T(2,128)S(1)} %dynamic-slice_bitcast_fusion.2, pred[768,5376]{1,0:T(8,128)(4,1)} %get-tuple-element.478), kind=kLoop, calls=%fused_computation.22.clone.1 | loop fusion | flops 49545216 | bytes 86716416 | tf_op jit(solution)/shard_map/while/body/eval_jaxpr/convert_element_type | solution.py:151
  917.4 17.6 %fusion.194 = f32[5376,64]{0,1:T(8,128)} fusion(f32[768,2,5376]{2,0,1:T(8,128)} %fusion.190, f32[2,768]{1,0:T(2,128)S(1)} %dynamic-slice_bitcast_fusion.2, pred[768,5376]{1,0:T(8,128)(4,1)} %get-tuple-element.478, f32[5376,64]{0,1:T(8,128)} %get-tuple-element.464, pred[]{:T(512)S(6)} %compare.116, bf16[6,768,2,64]{1,3,2,0:T(8,128)(2,1)} %get-tuple-element.482, ...), kind=kOutput, calls=%fused_computation.32.clone.1 | convolution fusion | flops 1090682880 | bytes 40114180 | tf_op jit(solution)/shard_map/while/body/eval_jaxpr/hqk,qhd->kd/dot_general | solution.py:161
  960.5 27.9 %fusion.191 = (f32[2,768]{1,0:T(2,128)S(1)}, f32[768,2,5376]{2,0,1:T(8,128)}) fusion(f32[768,2,5376]{2,0,1:T(8,128)} %fusion.190, f32[2,768]{1,0:T(2,128)S(1)} %dynamic-slice_bitcast_fusion.2, pred[768,5376]{1,0:T(8,128)(4,1)} %get-tuple-element.478, bf16[5376,64]{0,1:T(8,128)(2,1)S(1)} %copy-done.9, ...), kind=kOutput, calls=%fused_computation.20.clone.1 | convolution fusion | flops 1098250752 | bytes 71086080 | tf_op jit(solution)/shard_map/while/body/eval_jaxpr/qhd,kd->hqk/dot_general | solution.py:147
  988.4 28.7 %fusion.192 = bf16[2,768,5376]{2,1,0:T(8,128)(2,1)} fusion(f32[768,2,5376]{2,0,1:T(8,128)} %get-tuple-element.424, f32[768,2,5376]{2,0,1:T(8,128)} %fusion.190, f32[2,768]{1,0:T(2,128)S(1)} %get-tuple-element.425, f32[2,768]{1,0:T(2,128)S(1)} %dynamic-slice_bitcast_fusion.2, pred[768,5376]{1,0:T(8,128)(4,1)} %get-tuple-element.478), kind=kLoop, calls=%fused_computation.22.clone.1 | loop fusion | flops 49545216 | bytes 86716416 | tf_op jit(solution)/shard_map/while/body/eval_jaxpr/convert_element_type | solution.py:151
  1026.1 17.6 %fusion.194 = f32[5376,64]{0,1:T(8,128)} fusion(f32[768,2,5376]{2,0,1:T(8,128)} %fusion.190, f32[2,768]{1,0:T(2,128)S(1)} %dynamic-slice_bitcast_fusion.2, pred[768,5376]{1,0:T(8,128)(4,1)} %get-tuple-element.478, f32[5376,64]{0,1:T(8,128)} %get-tuple-element.464, pred[]{:T(512)S(6)} %compare.116, bf16[6,768,2,64]{1,3,2,0:T(8,128)(2,1)} %get-tuple-element.482, ...), kind=kOutput, calls=%fused_computation.32.clone.1 | convolution fusion | flops 1090682880 | bytes 40114180 | tf_op jit(solution)/shard_map/while/body/eval_jaxpr/hqk,qhd->kd/dot_general | solution.py:161
  1122.5 76.0 %all-reduce.1 = (f32[768]{0:T(1024)}, f32[768]{0:T(1024)}, f32[768]{0:T(1024)}, f32[64]{0:T(128)}, f32[768]{0:T(1024)}, /*index=5*/f32[768]{0:T(1024)}, f32[768]{0:T(1024)}, f32[3072]{0:T(1024)}, f32[768]{0:T(1024)}) all-reduce(f32[768]{0:T(1024)S(1)} %copy-done.58, ...), channel_id=1, replica_groups=mesh['seq'=16,'dp'=2] {'seq','dp'}, use_global_device_ids=true, to_apply=%region_23.24 | all-reduce | flops 8512 | bytes 68096 | tf_op jit(solution)/shard_map/psum | solution.py:190
  1198.4 313.3 %all-reduce.5.cloned.1.call-done = (f32[768,768]{1,0:T(8,128)}, f32[768,128]{1,0:T(8,128)}, f32[768,768]{1,0:T(8,128)}, f32[768,3072]{1,0:T(8,128)}, f32[3072,768]{1,0:T(8,128)}) async-done(((f32[768,768]{1,0:T(8,128)}, f32[768,128]{1,0:T(8,128)}, f32[768,768]{1,0:T(8,128)}, f32[768,3072]{1,0:T(8,128)}, f32[3072,768]{1,0:T(8,128)}), (f32[768,768]{1,0:T(8,128)}, f32[768,128]{1,0:T(8,128)}, ...) | async-done | bytes 23986192 | tf_op jit(solution)/shard_map/psum | solution.py:190
  (317 shorter events, 516.3 us)
Async XLA Ops:
  7.2 348.1 %copy-start = (bf16[768,768]{1,0:T(8,128)(2,1)S(1)}, bf16[768,768]{1,0:T(8,128)(2,1)}, u32[]{:S(2)}) copy-start(bf16[768,768]{1,0:T(8,128)(2,1)} %param.30) | copy-start | bytes 3538948
  7.2 1504.5 %all-reduce.5.cloned.1.call-start = ((), (), s32[]{:S(2)}) async-start(), calls=%async_computation | async-start | bytes 47972352 | tf_op jit(solution)/shard_map/psum | solution.py:190
  10.7 29.4 %copy-start.15 = (bf16[768,768]{0,1:T(8,128)(2,1)}, bf16[768,768]{0,1:T(8,128)(2,1)S(1)}, u32[]{:S(2)}) copy-start(bf16[768,768]{0,1:T(8,128)(2,1)S(1)} %fusion.66) | copy-start | bytes 3538948
  12.0 40.1 %collective-permute-start = (bf16[768,128]{1,0:T(8,128)(2,1)}, bf16[768,128]{1,0:T(8,128)(2,1)}, u32[]{:S(2)}, u32[]{:S(2)}) collective-permute-start(bf16[768,128]{1,0:T(8,128)(2,1)} %get-tuple-element.292), channel_id=1, source_target_pairs={{0,2},{2,4},{4,6},{6,8},{8,10},{10,12},{12,14},{14,16},{16,18},{18... | collective-permute-start | bytes 589832 | tf_op jit(solution)/shard_map/ppermute | solution.py:18
  17.5 37.0 %collective-permute-start.1 = (bf16[768,128]{1,0:T(8,128)(2,1)}, bf16[768,128]{1,0:T(8,128)(2,1)}, u32[]{:S(2)}, u32[]{:S(2)}) collective-permute-start(bf16[768,128]{1,0:T(8,128)(2,1)} %get-tuple-element.292), channel_id=1, source_target_pairs={{0,4},{2,6},{4,8},{6,10},{8,12},{10,14},{12,16},{14,18},{16,20},{1... | collective-permute-start | bytes 589832 | tf_op jit(solution)/shard_map/ppermute | solution.py:18
  20.9 34.6 %collective-permute-start.2 = (bf16[768,128]{1,0:T(8,128)(2,1)}, bf16[768,128]{1,0:T(8,128)(2,1)}, u32[]{:S(2)}, u32[]{:S(2)}) collective-permute-start(bf16[768,128]{1,0:T(8,128)(2,1)} %get-tuple-element.292), channel_id=1, source_target_pairs={{0,6},{2,8},{4,10},{6,12},{8,14},{10,16},{12,18},{14,20},{16,22},{... | collective-permute-start | bytes 589832 | tf_op jit(solution)/shard_map/ppermute | solution.py:18
  25.3 31.2 %collective-permute-start.3 = (bf16[768,128]{1,0:T(8,128)(2,1)}, bf16[768,128]{1,0:T(8,128)(2,1)}, u32[]{:S(2)}, u32[]{:S(2)}) collective-permute-start(bf16[768,128]{1,0:T(8,128)(2,1)} %get-tuple-element.292), channel_id=1, source_target_pairs={{0,8},{2,10},{4,12},{6,14},{8,16},{10,18},{12,20},{14,22},{16,24},... | collective-permute-start | bytes 589832 | tf_op jit(solution)/shard_map/ppermute | solution.py:18
  28.8 28.7 %collective-permute-start.4 = (bf16[768,128]{1,0:T(8,128)(2,1)}, bf16[768,128]{1,0:T(8,128)(2,1)}, u32[]{:S(2)}, u32[]{:S(2)}) collective-permute-start(bf16[768,128]{1,0:T(8,128)(2,1)} %get-tuple-element.292), channel_id=1, source_target_pairs={{0,10},{2,12},{4,14},{6,16},{8,18},{10,20},{12,22},{14,24},{16,26}... | collective-permute-start | bytes 589832 | tf_op jit(solution)/shard_map/ppermute | solution.py:18
  43.0 10.5 copy-start.18
  52.0 6.4 collective-permute-start.5
  64.8 290.6 %copy-start.3 = (bf16[1,768,768]{1,2,0:T(8,128)(2,1)S(1)}, bf16[1,768,768]{1,2,0:T(8,128)(2,1)}, u32[]{:S(2)}) copy-start(bf16[1,768,768]{1,2,0:T(8,128)(2,1)} %copy-done.2) | copy-start | bytes 3538948
  64.8 290.6 %copy-start.66 = (f32[768]{0:T(1024)S(1)}, f32[768]{0:T(1024)}, u32[]{:S(2)}) copy-start(f32[768]{0:T(1024)} %param.31) | copy-start | bytes 9220
  358.1 39.9 %copy-start.33 = (f32[768]{0:T(1024)}, f32[768]{0:T(1024)S(1)}, u32[]{:S(2)}) copy-start(f32[768]{0:T(1024)S(1)} %broadcast_multiply_fusion) | copy-start | bytes 9220
  359.5 38.5 %copy-start.36 = (f32[768]{0:T(1024)}, f32[768]{0:T(1024)S(1)}, u32[]{:S(2)}) copy-start(f32[768]{0:T(1024)S(1)} %fusion.124) | copy-start | bytes 9220
  359.5 12.4 slice-start.5
  403.7 14.1 copy-start.9
  512.0 14.1 copy-start.9
  620.6 14.1 copy-start.9
  729.2 14.1 copy-start.9
  837.8 14.1 copy-start.9
  946.5 14.1 copy-start.9
  1057.0 16.0 %copy-start.28 = (bf16[6,768,2,64]{1,3,2,0:T(8,128)(2,1)S(1)}, bf16[6,768,2,64]{1,3,2,0:T(8,128)(2,1)}, u32[]{:S(2)}) copy-start(bf16[6,768,2,64]{1,3,2,0:T(8,128)(2,1)} %get-tuple-element.108) | copy-start | bytes 3538948
  1057.0 16.0 %copy-start.30 = (bf16[768,768]{0,1:T(8,128)(2,1)S(1)}, bf16[768,768]{0,1:T(8,128)(2,1)}, u32[]{:S(2)}) copy-start(bf16[768,768]{0,1:T(8,128)(2,1)} %copy-done.29) | copy-start | bytes 3538948
  1057.0 14.4 collective-permute-start.11
  1066.3 21.5 %collective-permute-start.10 = (f32[768,128]{0,1:T(8,128)S(1)}, f32[768,128]{0,1:T(8,128)S(1)}, u32[]{:S(2)}, u32[]{:S(2)}) collective-permute-start(f32[768,128]{0,1:T(8,128)S(1)} %get-tuple-element.283), channel_id=1, source_target_pairs={{10,0},{12,2},{14,4},{16,6},{18,8},{20,10},{22,12},{24,14},{26,16}... | collective-permute-start | bytes 1179656 | tf_op jit(solution)/shard_map/ppermute | solution.py:18
  1067.6 27.8 %collective-permute-start.9 = (f32[768,128]{0,1:T(8,128)S(1)}, f32[768,128]{0,1:T(8,128)S(1)}, u32[]{:S(2)}, u32[]{:S(2)}) collective-permute-start(f32[768,128]{0,1:T(8,128)S(1)} %get-tuple-element.284), channel_id=1, source_target_pairs={{8,0},{10,2},{12,4},{14,6},{16,8},{18,10},{20,12},{22,14},{24,16},... | collective-permute-start | bytes 1179656 | tf_op jit(solution)/shard_map/ppermute | solution.py:18
  1068.9 26.5 %collective-permute-start.8 = (f32[768,128]{0,1:T(8,128)S(1)}, f32[768,128]{0,1:T(8,128)S(1)}, u32[]{:S(2)}, u32[]{:S(2)}) collective-permute-start(f32[768,128]{0,1:T(8,128)S(1)} %get-tuple-element.285), channel_id=1, source_target_pairs={{6,0},{8,2},{10,4},{12,6},{14,8},{16,10},{18,12},{20,14},{22,16},{... | collective-permute-start | bytes 1179656 | tf_op jit(solution)/shard_map/ppermute | solution.py:18
  1070.2 25.2 %collective-permute-start.7 = (f32[768,128]{0,1:T(8,128)S(1)}, f32[768,128]{0,1:T(8,128)S(1)}, u32[]{:S(2)}, u32[]{:S(2)}) collective-permute-start(f32[768,128]{0,1:T(8,128)S(1)} %get-tuple-element.286), channel_id=1, source_target_pairs={{4,0},{6,2},{8,4},{10,6},{12,8},{14,10},{16,12},{18,14},{20,16},{2... | collective-permute-start | bytes 1179656 | tf_op jit(solution)/shard_map/ppermute | solution.py:18
  1071.5 23.9 %collective-permute-start.6 = (f32[768,128]{0,1:T(8,128)S(1)}, f32[768,128]{0,1:T(8,128)S(1)}, u32[]{:S(2)}, u32[]{:S(2)}) collective-permute-start(f32[768,128]{0,1:T(8,128)S(1)} %get-tuple-element.281), channel_id=1, source_target_pairs={{2,0},{4,2},{6,4},{8,6},{10,8},{12,10},{14,12},{16,14},{18,16},{20... | collective-permute-start | bytes 1179656 | tf_op jit(solution)/shard_map/ppermute | solution.py:18
  1078.3 18.0 %copy-start.16 = (bf16[768,768]{0,1:T(8,128)(2,1)S(1)}, bf16[768,768]{0,1:T(8,128)(2,1)}, u32[]{:S(2)}) copy-start(bf16[768,768]{0,1:T(8,128)(2,1)} %copy-done.15) | copy-start | bytes 3538948
  1515.8 10.7 slice-start
  1517.2 9.3 slice-start.2
  (63 other events, 199.5 us)
Sparse Core Ops, SparseCore 0:
  1097.6 414.0 all-reduce.4
where the time goes:
time: 1550 us; the launch traced here: 1540 us
  matrix products  740 us (48%)
  waiting for transfers between devices  330 us (21%)
  other arithmetic  295 us (19%)
  blocking collectives  76 us (5%)
  local copies, waits for them, and re-layouts  50.4 us (3%)
  starting transfers between devices  30 us (2%)
  between operations  15.5 us (1%)
    psum x1, waiting for transfers between devices, per_device(): lax.psum((grad_gain_one, grad_shift_one, grad_qw, grad_qb, grad_kvw, grad...  313 us
    convert_element_type x6, other arithmetic, backward_pair(): grad_scores = (probability * centered).astype(jnp.bfloat16)  172 us
    dot_general x12, matrix products, scores_of(): jnp.einsum('qhd,kd->hqk', query_pair, key_part, preferred_element_type=jn...  171 us
    dot_general x6, matrix products, backward_pair(): jnp.einsum('qhd,kd->hqk', grad_pair, val_part, preferred_element_type=jnp...  167 us
    dot_general x6, matrix products, forward_pair(): jnp.einsum('hqk,kd->qhd', prob_low, val_part, preferred_element_type=jnp....  105 us
    dot_general x6, matrix products, backward_pair(): jnp.einsum('hqk,qhd->kd', prob_low, grad_pair, preferred_element_type=jnp...  105 us
    reduce_sum x6, other arithmetic, forward_pair(): row_total = jnp.sum(exponent, axis=-1, keepdims=True)  98 us
    psum x1, blocking collectives, per_device(): lax.psum((grad_gain_one, grad_shift_one, grad_qw, grad_qb, grad_kvw, grad...  76 us
  transfers between devices with their start and end apart: 13, of which 3 were waited for; matrix products, arithmetic and copies ran while one was open for 4% of the time, Pallas kernels for 0%

commit v1 on v0

v1 whole, which is shorter than its diff:
```python
from functools import partial

import jax
import jax.numpy as jnp
import numpy as np
from jax import lax
from jax.experimental import pallas as pl
from jax.experimental.pallas import tpu as pltpu
from jax.sharding import PartitionSpec as P

ROW = 4096
CHUNK = 128
BLOCK = 512
PAD = BLOCK - CHUNK
LOG2E = 1.4426950408889634
BIG = -1e30
SAFE = 60.0
epsilon = 1e-05
bf16 = jnp.bfloat16
f32 = jnp.float32

TRIPLES = (0, 2, 4, 3, 1, 5, 6, 8, 9, 7, 10, 12, 14, 15, 13, 11)


class Plan:
    def __init__(self, devices, shard_len):
        self.devices = devices
        self.per_dev = shard_len // CHUNK
        per_row = ROW // CHUNK
        half = per_row // 2
        pairs = self.per_dev // 2
        unit = len(TRIPLES)
        assert devices % unit == 0 and shard_len * unit % ROW == 0
        self.work = np.zeros((devices, self.per_dev), np.int32)
        for dev in range(devices):
            triple = dev // unit * unit + TRIPLES[dev % unit]
            for i in range(pairs):
                row, c = divmod(triple * pairs + i, half)
                self.work[dev, i] = row * per_row + c
                self.work[dev, pairs + i] = row * per_row + per_row - 1 - c
        self.row = self.work // per_row
        self.slot = self.work % per_row
        self.first_row = self.row.min(axis=1)
        self.last_row = self.row.max(axis=1)
        self.row_sel = self.row - self.first_row[:, None]
        moves = []
        self.pick = np.zeros((devices, self.per_dev), np.int32)
        for dev in range(devices):
            for slot in range(self.per_dev):
                src, chunk = divmod(int(self.work[dev, slot]), self.per_dev)
                if src == dev:
                    self.pick[dev, slot] = chunk
                else:
                    moves.append((src, chunk, dev, slot))
        degree = max(
            max(sum(m[0] == d for m in moves), sum(m[2] == d for m in moves)) for d in range(devices)
        )
        self.colors = [[] for _ in range(degree)]
        out_used = [dict() for _ in range(devices)]
        in_used = [dict() for _ in range(devices)]
        for move in moves:
            s, t = move[0], move[2]
            a = next(k for k in range(degree) if k not in out_used[s])
            b = next(k for k in range(degree) if k not in in_used[t])
            if a != b and a in in_used[t]:
                node, side, path = t, "in", []
                want = a
                while True:
                    used = in_used[node] if side == "in" else out_used[node]
                    if want not in used:
                        break
                    edge = used[want]
                    path.append((edge, want))
                    node = edge[0] if side == "in" else edge[2]
                    side = "out" if side == "in" else "in"
                    want = b if want == a else a
                for edge, k in path:
                    del out_used[edge[0]][k]
                    del in_used[edge[2]][k]
                for edge, k in path:
                    other = b if k == a else a
                    out_used[edge[0]][other] = edge
                    in_used[edge[2]][other] = edge
            out_used[s][a] = move
            in_used[t][a] = move
        self.send_chunk = np.zeros((degree, devices), np.int32)
        self.send_slot = np.zeros((degree, devices), np.int32)
        self.back = np.zeros((devices, self.per_dev), np.int32)
        for dev in range(devices):
            for k, m in in_used[dev].items():
                self.pick[dev, m[3]] = self.per_dev + k
                self.send_slot[k, dev] = m[3]
            for k, m in out_used[dev].items():
                self.colors[k].append((m[0], m[2]))
                self.send_chunk[k, dev] = m[1]
                self.back[dev, m[1]] = self.per_dev + k
            for slot in range(self.per_dev):
                src, chunk = divmod(int(self.work[dev, slot]), self.per_dev)
                if src == dev:
                    self.back[dev, chunk] = slot
        self.degree = degree
        rows_of = [
            set(range(d * shard_len // ROW, ((d + 1) * shard_len - 1) // ROW + 1))
            for d in range(devices)
        ]
        self.reach = 0
        for d in range(devices):
            for e in range(devices):
                if rows_of[d] & rows_of[e]:
                    self.reach = max(self.reach, abs(d - e))
        self.share = {
            off: [
                (d, d + off)
                for d in range(devices)
                if 0 <= d + off < devices and rows_of[d] & rows_of[d + off]
            ]
            for off in range(-self.reach, self.reach + 1)
        }


def take_chunks(options, index):
    count = index.shape[0]
    return jnp.concatenate(
        [lax.dynamic_slice_in_dim(options, index[i] * CHUNK, CHUNK, 0) for i in range(count)], axis=0
    )


def to_work(plan, device, value):
    received = [
        lax.ppermute(
            lax.dynamic_slice_in_dim(
                value, jnp.asarray(plan.send_chunk[k])[device] * CHUNK, CHUNK, 0
            ),
            "seq",
            plan.colors[k],
        )
        for k in range(plan.degree)
    ]
    return take_chunks(jnp.concatenate([value] + received, axis=0), jnp.asarray(plan.pick)[device])


def to_home(plan, device, value):
    received = [
        lax.ppermute(
            lax.dynamic_slice_in_dim(
                value, jnp.asarray(plan.send_slot[k])[device] * CHUNK, CHUNK, 0
            ),
            "seq",
            [(b, a) for a, b in plan.colors[k]],
        )
        for k in range(plan.degree)
    ]
    return take_chunks(jnp.concatenate([value] + received, axis=0), jnp.asarray(plan.back)[device])


def normed(values, gains, shifts):
    center = values - jnp.mean(values, axis=-1, keepdims=True)
    spread = jnp.mean(center * center, axis=-1, keepdims=True)
    return center * lax.rsqrt(spread + epsilon) * gains + shifts


def contract(left_op, right_op, left_dim, right_dim):
    return lax.dot_general(
        left_op, right_op, (((left_dim,), (right_dim,)), ((), ())), preferred_element_type=f32
    )


def wide(block, heads, head_dim):
    return jnp.concatenate([block[h * head_dim : (h + 1) * head_dim] for h in range(heads)], axis=1)


def tall(block, heads):
    return jnp.concatenate([block[:, h * CHUNK : (h + 1) * CHUNK] for h in range(heads)], axis=0)


def hi_lo(value, count):
    parts = []
    for _ in range(count):
        part = value.astype(bf16)
        parts.append(part)
        value = value - part.astype(f32)
    return parts


def scaled_queries(q_block, heads, head_dim, extra):
    q = wide(q_block, heads, head_dim)
    hi, lo = hi_lo(q.astype(f32) * (LOG2E * head_dim ** (-0.5)), 2)
    width = q.shape[1]
    ones = jnp.ones((1, width), f32)
    rows = jnp.concatenate(
        extra + [ones, jnp.zeros((2 * head_dim - 1 - len(extra), width), f32)], axis=0
    ).astype(bf16)
    return q, jnp.concatenate([hi, lo, rows], axis=0)


def triangle(heads):
    key = lax.broadcasted_iota(jnp.int32, (CHUNK, heads * CHUNK), 0)
    query = lax.broadcasted_iota(jnp.int32, (CHUNK, heads * CHUNK), 1) % CHUNK
    return key <= query


def first_scores(k_block, q_aug, heads):
    s = contract(k_block, q_aug, 1, 0)
    return jnp.concatenate([s[:PAD], jnp.where(triangle(heads), s[PAD:], BIG)], axis=0)


def attend_kernel(heads, head_dim, meta, q_ref, k_ref, vt_ref, o_ref, lse_ref, acc, top):
    i = pl.program_id(0)
    n = pl.num_programs(0)
    row = meta[i]
    end = (meta[n + i] + 1) * CHUNK + PAD
    blocks = meta[n + i] // (BLOCK // CHUNK) + 1
    zero = jnp.zeros((1, heads * CHUNK), f32)
    _, q_aug = scaled_queries(q_ref[...], heads, head_dim, [zero, zero, zero])

    def scores(j):
        off = pl.multiple_of(end - (j + 1) * BLOCK, CHUNK)
        return contract(k_ref[row, pl.ds(off, BLOCK), :], q_aug, 1, 0)

    def values(j):
        off = pl.multiple_of(end - (j + 1) * BLOCK, CHUNK)
        return vt_ref[row, :, pl.ds(off, BLOCK)]

    def masked(s):
        return jnp.concatenate([s[:PAD], jnp.where(triangle(heads), s[PAD:], BIG)], axis=0)

    @pl.when(meta[2 * n] > 0)
    def _():
        p = jnp.exp2(masked(scores(0))).astype(bf16)
        acc[...] = contract(values(0), p, 1, 0)

        def step(j, _):
            p = jnp.exp2(scores(j)).astype(bf16)
            acc[...] += contract(values(j), p, 1, 0)
            return 0

        lax.fori_loop(1, blocks, step, 0)
        top[...] = jnp.zeros_like(top)

    @pl.when(meta[2 * n] == 0)
    def _():
        s = masked(scores(0))
        m = jnp.max(s, axis=0, keepdims=True)
        top[...] = m
        acc[...] = contract(values(0), jnp.exp2(s - m).astype(bf16), 1, 0)

        def step(j, _):
            s = scores(j)
            old = top[...]
            m = jnp.maximum(old, jnp.max(s, axis=0, keepdims=True))
            top[...] = m
            p = jnp.exp2(s - m).astype(bf16)
            acc[...] = acc[...] * jnp.exp2(old - m) + contract(values(j), p, 1, 0)
            return 0

        lax.fori_loop(1, blocks, step, 0)

    total = acc[head_dim : head_dim + 1, :]
    o_ref[...] = tall(acc[:head_dim, :] / total, heads).astype(bf16)
    lse_ref[0] = top[...] + jnp.log2(total)


def back_kernel(
    heads, head_dim, meta, q_ref, g_ref, o_ref, lse_ref, k_ref, v_ref, kt_ref, dq_ref, dkv_ref, acc
):
    i = pl.program_id(0)
    n = pl.num_programs(0)
    row = meta[i]
    end = (meta[n + i] + 1) * CHUNK + PAD
    blocks = meta[n + i] // (BLOCK // CHUNK) + 1

    @pl.when(i == 0)
    def _():
        dkv_ref[...] = jnp.zeros_like(dkv_ref)

    lse_parts = [part.astype(f32) for part in hi_lo(-lse_ref[0], 3)]
    q, q_aug = scaled_queries(q_ref[...], heads, head_dim, lse_parts)
    g = wide(g_ref[...], heads, head_dim)
    o = wide(o_ref[...], heads, head_dim)
    delta = jnp.sum(g.astype(f32) * o.astype(f32), axis=0, keepdims=True)
    delta_parts = [part.astype(f32) for part in hi_lo(-delta, 3)]
    fill = jnp.zeros((head_dim - 3, heads * CHUNK), f32)
    g_aug = jnp.concatenate([g, jnp.concatenate(delta_parts + [fill], axis=0).astype(bf16)], axis=0)

    def block(j, first):
        off = pl.multiple_of(end - (j + 1) * BLOCK, CHUNK)
        at = pl.ds(off, BLOCK)
        s = contract(k_ref[row, at, :], q_aug, 1, 0)
        if first:
            s = jnp.concatenate([s[:PAD], jnp.where(triangle(heads), s[PAD:], BIG)], axis=0)
        dp = contract(v_ref[row, at, :], g_aug, 1, 0)
        p = jnp.exp2(s)
        ds = (p * dp).astype(bf16)
        p = p.astype(bf16)
        dq = contract(kt_ref[row, :, at], ds, 1, 0)
        if first:
            acc[...] = dq
        else:
            acc[...] += dq
        dkv_ref[row, :head_dim, at] += contract(q, ds, 1, 1)
        dkv_ref[row, head_dim:, at] += contract(g, p, 1, 1)

    block(0, True)

    def step(j, _):
        block(j, False)
        return 0

    lax.fori_loop(1, blocks, step, 0)
    dq_ref[...] = tall(acc[...] * head_dim ** (-0.5), heads).astype(bf16)

    @pl.when(i == n - 1)
    def _():
        dkv_ref[:, :head_dim] = dkv_ref[:, :head_dim] * head_dim ** (-0.5)


def whole(shape):
    return pl.BlockSpec(shape, lambda i, meta: (0,) * len(shape))


def column(rows):
    return pl.BlockSpec((rows, CHUNK), lambda i, meta: (0, i))


def lead(shape):
    return pl.BlockSpec((1,) + shape, lambda i, meta: (i,) + (0,) * len(shape))


def per_device(
    plan,
    tokens,
    lengths,
    cotangent,
    norm1_gain,
    norm1_shift,
    query_weight,
    query_bias,
    keyval_weight,
    value_bias,
    out_weight,
    out_bias,
    norm2_gain,
    norm2_shift,
    up_weight,
    up_bias,
    down_weight,
    down_bias,
):
    device = lax.axis_index("seq")
    shard_len, width = tokens.shape[1:]
    head_dim = keyval_weight.shape[1] // 2
    heads = width // head_dim
    columns = heads * CHUNK
    chunks = plan.per_dev
    limit = dict(vmem_limit_bytes=56 * 2**20)

    home_tokens = tokens[0]
    home_inputs = home_tokens.astype(f32)
    normal_home = normed(home_inputs, norm1_gain, norm1_shift).astype(bf16)
    kv_bias = jnp.concatenate([jnp.zeros((head_dim,), f32), value_bias])
    keyvals = (contract(normal_home, keyval_weight, 1, 0) + kv_bias).astype(bf16)

    reach = plan.reach
    window = jnp.concatenate(
        [
            keyvals if off == 0 else lax.ppermute(keyvals, "seq", plan.share[-off])
            for off in range(-reach, reach + 1)
        ],
        axis=0,
    )
    origin = (device - reach) * shard_len
    row_ids = jnp.stack([jnp.asarray(plan.first_row)[device], jnp.asarray(plan.last_row)[device]])
    starts = row_ids * ROW - origin
    key_slot = jnp.arange(ROW + PAD, dtype=jnp.int32) - PAD
    k_aug, v_aug, vt_aug, kt_all = [], [], [], []
    for r in range(2):
        rows = lax.dynamic_slice_in_dim(window, starts[r], ROW, 0)
        rows = jnp.concatenate([jnp.zeros((PAD, 2 * head_dim), bf16), rows], axis=0)
        keys, vals = rows[:, :head_dim], rows[:, head_dim:]
        live = (key_slot >= 0) & (key_slot < lengths[0][row_ids[r]])
        bias = jnp.where(live, 0.0, BIG).astype(bf16)[:, None]
        ones = jnp.ones((ROW + PAD, 3), bf16)
        k_aug.append(
            jnp.concatenate(
                [keys, keys, ones, bias, jnp.zeros((ROW + PAD, 2 * head_dim - 4), bf16)], axis=1
            )
        )
        v_aug.append(
            jnp.concatenate([vals, ones, jnp.zeros((ROW + PAD, head_dim - 3), bf16)], axis=1)
        )
        vt_aug.append(
            jnp.concatenate(
                [vals.T, jnp.ones((1, ROW + PAD), bf16), jnp.zeros((15, ROW + PAD), bf16)], axis=0
            )
        )
        kt_all.append(keys.T)
    k_aug, v_aug, vt_aug, kt_all = map(jnp.stack, (k_aug, v_aug, vt_aug, kt_all))

    work_tokens = to_work(plan, device, home_tokens)
    upstream = to_work(plan, device, cotangent[0])
    inputs = work_tokens.astype(f32)
    normal_one = normed(inputs, norm1_gain, norm1_shift).astype(bf16)
    queries = (contract(query_weight, normal_one, 0, 1) + query_bias[:, None]).astype(bf16)

    q_norm = jnp.max(jnp.sum(jnp.square(queries.astype(f32).reshape(heads, head_dim, -1)), axis=1))
    k_norm = jnp.max(jnp.sum(jnp.square(window[:, :head_dim].astype(f32)), axis=1))
    bound = jnp.sqrt(q_norm * k_norm) * (LOG2E * head_dim ** (-0.5))
    meta = jnp.concatenate(
        [
            jnp.asarray(plan.row_sel)[device],
            jnp.asarray(plan.slot)[device],
            (bound < SAFE).astype(jnp.int32)[None],
        ]
    )

    key_rows = ROW + PAD
    attended, lse = pl.pallas_call(
        partial(attend_kernel, heads, head_dim),
        grid_spec=pltpu.PrefetchScalarGridSpec(
            num_scalar_prefetch=1,
            grid=(chunks,),
            in_specs=[
                column(width),
                whole((2, key_rows, 4 * head_dim)),
                whole((2, head_dim + 16, key_rows)),
            ],
            out_specs=[column(width), lead((1, columns))],
            scratch_shapes=[pltpu.VMEM((head_dim + 16, columns), f32), pltpu.VMEM((1, columns), f32)],
        ),
        out_shape=[
            jax.ShapeDtypeStruct((width, shard_len), bf16),
            jax.ShapeDtypeStruct((chunks, 1, columns), f32),
        ],
        compiler_params=pltpu.CompilerParams(**limit),
        name="attend",
    )(meta, queries, k_aug, vt_aug)

    residual = inputs + contract(attended, out_weight, 0, 0) + out_bias
    normal_two = normed(residual, norm2_gain, norm2_shift).astype(bf16)
    hidden_pre = contract(normal_two, up_weight, 1, 0) + up_bias
    activated = jax.nn.gelu(hidden_pre, approximate=True).astype(bf16)
    outputs = (residual + contract(activated, down_weight, 1, 0) + down_bias).astype(bf16)
    outputs = to_home(plan, device, outputs)
    upstream_wide = upstream.astype(f32)
    grad_down = contract(activated, upstream, 0, 0)
    grad_down_bias = jnp.sum(upstream_wide, axis=0)
    grad_act = contract(upstream, down_weight, 1, 1)
    _, gelu_back = jax.vjp(partial(jax.nn.gelu, approximate=True), hidden_pre)
    grad_hidden = gelu_back(grad_act)[0].astype(bf16)
    grad_up = contract(normal_two, grad_hidden, 0, 0)
    grad_up_bias = jnp.sum(grad_hidden.astype(f32), axis=0)
    grad_normal_two = contract(grad_hidden, up_weight, 1, 1)
    _, norm_two_back = jax.vjp(normed, residual, norm2_gain, norm2_shift)
    grad_res_part, grad_gain_two, grad_shift_two = norm_two_back(grad_normal_two)
    grad_residual = upstream_wide + grad_res_part
    grad_proj = grad_residual.astype(bf16)
    grad_out_w = contract(attended, grad_proj, 1, 0)
    grad_out_b = jnp.sum(grad_proj.astype(f32), axis=0)
    grad_att = contract(out_weight, grad_proj, 1, 1).astype(bf16)
    home_residual = to_home(plan, device, grad_proj).astype(f32)

    grad_queries, grad_rows = pl.pallas_call(
        partial(back_kernel, heads, head_dim),
        grid_spec=pltpu.PrefetchScalarGridSpec(
            num_scalar_prefetch=1,
            grid=(chunks,),
            in_specs=[
                column(width),
                column(width),
                column(width),
                lead((1, columns)),
                whole((2, key_rows, 4 * head_dim)),
                whole((2, key_rows, 2 * head_dim)),
                whole((2, head_dim, key_rows)),
            ],
            out_specs=[column(width), whole((2, 2 * head_dim, key_rows))],
            scratch_shapes=[pltpu.VMEM((head_dim, columns), f32)],
        ),
        out_shape=[
            jax.ShapeDtypeStruct((width, shard_len), bf16),
            jax.ShapeDtypeStruct((2, 2 * head_dim, key_rows), f32),
        ],
        compiler_params=pltpu.CompilerParams(**limit),
        name="attend_back",
    )(meta, queries, grad_att, attended, lse, k_aug, v_aug, kt_all)

    grad_window = jnp.zeros(((2 * reach + 1) * shard_len, 2 * head_dim), f32)
    same = row_ids[0] == row_ids[1]
    for r in range(2):
        part = grad_rows[r][:, PAD:].T
        if r == 1:
            part = jnp.where(same, 0.0, part)
        old = lax.dynamic_slice_in_dim(grad_window, starts[r], ROW, 0)
        grad_window = lax.dynamic_update_slice_in_dim(grad_window, old + part, starts[r], 0)
    grad_window = grad_window.astype(bf16)
    returned = jnp.zeros((shard_len, 2 * head_dim), f32)
    for off in range(-reach, reach + 1):
        piece = grad_window[(off + reach) * shard_len : (off + reach + 1) * shard_len]
        if off != 0:
            piece = lax.ppermute(piece, "seq", plan.share[off])
        returned = returned + piece.astype(f32)
    grad_kv = returned.astype(bf16)

    grad_queries_home = to_home(plan, device, grad_queries.T)
    grad_qw = contract(normal_one, grad_queries, 0, 1)
    grad_qb = jnp.sum(grad_queries.astype(f32), axis=1)
    grad_kvw = contract(normal_home, grad_kv, 0, 0)
    grad_vb = jnp.sum(grad_kv[:, head_dim:].astype(f32), axis=0)
    grad_normal_one = contract(grad_queries_home, query_weight, 1, 1) + contract(
        grad_kv, keyval_weight, 1, 1
    )
    _, norm_one_back = jax.vjp(normed, home_inputs, norm1_gain, norm1_shift)
    grad_in_part, grad_gain_one, grad_shift_one = norm_one_back(grad_normal_one)
    grad_inputs = home_residual + grad_in_part
    big = (grad_qw, grad_kvw, grad_out_w, grad_up, grad_down)
    small = (
        grad_gain_one,
        grad_shift_one,
        grad_qb,
        grad_vb,
        grad_out_b,
        grad_gain_two,
        grad_shift_two,
        grad_up_bias,
        grad_down_bias,
    )
    sizes = np.cumsum([v.shape[0] for v in small])[:-1]
    small = jnp.split(lax.psum(jnp.concatenate(small), ("seq", "dp")), sizes)
    big = [
        v.astype(f32) for v in lax.psum(tuple(v.astype(bf16) for v in big), ("seq", "dp"))
    ]
    gain_one, shift_one, qb, vb, out_b, gain_two, shift_two, up_b, down_b = small
    qw, kvw, out_w, up_w, down_w = big
    return (
        outputs[None],
        grad_inputs[None],
        gain_one,
        shift_one,
        qw,
        qb,
        kvw,
        vb,
        out_w,
        out_b,
        gain_two,
        shift_two,
        up_w,
        up_b,
        down_w,
        down_b,
    )


def solution(mesh):
    split = P("dp", "seq", None)
    devices = mesh.shape["seq"]

    def run(*arrays):
        plan = Plan(devices, arrays[0].shape[1] // devices)
        return jax.shard_map(
            partial(per_device, plan),
            mesh=mesh,
            in_specs=(split, P("dp", None), split) + (P(),) * 14,
            out_specs=(split, split) + (P(),) * 14,
            check_vma=False,
        )(*arrays)

    return run
```

time: 1550 us -> 767 us (0.49)
  matrix products: 740 us -> 74.9 us
  other arithmetic: 295 us -> 59.3 us
  waiting for transfers between devices: 330 us -> 166 us
  starting transfers between devices: 30 us -> 140 us
  Pallas kernels: 0 us -> 94.3 us
  local copies, waits for them, and re-layouts: 50.4 us -> 132 us
  blocking collectives: 76 us -> 50.2 us
  between operations: 15.5 us -> 40.6 us
    dot_general x57 -> x15, matrix products: 740 us -> 74.9 us  [contract(): lax.dot_general(left_op, right_op, (((left_dim,), (right_dim,)), ((), ())...]
    psum x1, waiting for transfers between devices: 313 us -> 119 us  [per_device(): lax.psum(tuple((v.astype(bf16) for v in big)), ('seq', 'dp'))]
    convert_element_type x8 -> x10, other arithmetic: 173 us -> 23.6 us  [the longest x5 15.9 us: per_device(): v.astype(f32)]
    ppermute x12 -> x45, starting transfers between devices: 30 us -> 140 us  [the longest x15 54.1 us: to_home(): lax.ppermute(lax.dynamic_slice_in_dim(value, jnp.asarray(plan.send_slot[k...]
    reduce_sum x11 -> x5, other arithmetic: 101 us -> 5.88 us  [the longest x1 2.47 us: per_device(): jnp.sum(jnp.square(queries.astype(f32).reshape(heads, head_dim, -1)), axi...]
    pallas_call x0 -> x2, Pallas kernels: none -> 94.3 us  [the longest x1 66.9 us: per_device(): pl.pallas_call(partial(back_kernel, heads, head_dim), grid_spec=pltpu.Pre...]
    ppermute x12 -> x45, waiting for transfers between devices: 17.2 us -> 46.7 us  [the longest x10 27.4 us: to_work(): lax.ppermute(lax.dynamic_slice_in_dim(value, jnp.asarray(plan.send_chunk[...]
    psum x1, blocking collectives: 76 us -> 50.2 us  [per_device(): small = jnp.split(lax.psum(jnp.concatenate(small), ('seq', 'dp')), sizes)]
  transfers between devices with their start and end apart: 13 -> 46, of which waited for: 3 -> 12; matrix products, arithmetic and copies ran while one was open for 4% -> 11% of each run, Pallas kernels for 0% -> 0%
where the time goes in v1:
time: 767 us; the launch traced here: 757 us
  waiting for transfers between devices  166 us (22%)
  starting transfers between devices  140 us (18%)
  local copies, waits for them, and re-layouts  132 us (17%)
  Pallas kernels  94.3 us (12%)
  matrix products  74.9 us (10%)
  other arithmetic  59.3 us (8%)
  blocking collectives  50.2 us (7%)
  between operations  40.6 us (5%)
    psum x1, waiting for transfers between devices, per_device(): lax.psum(tuple((v.astype(bf16) for v in big)), ('seq', 'dp'))  119 us
    dot_general x15, matrix products, contract(): lax.dot_general(left_op, right_op, (((left_dim,), (right_dim,)), ((), ())...  74.9 us
    pallas_call x1, Pallas kernels, per_device(): pl.pallas_call(partial(back_kernel, heads, head_dim), grid_spec=pltpu.Pre...  66.9 us
    ppermute x15, starting transfers between devices, to_home(): lax.ppermute(lax.dynamic_slice_in_dim(value, jnp.asarray(plan.send_slot[k...  54.1 us
    psum x1, blocking collectives, per_device(): small = jnp.split(lax.psum(jnp.concatenate(small), ('seq', 'dp')), sizes)  50.2 us
    unnamed x199, local copies, waits for them, and re-layouts  39.9 us
    ppermute x10, starting transfers between devices, to_work(): lax.ppermute(lax.dynamic_slice_in_dim(value, jnp.asarray(plan.send_chunk[...  31.2 us
    ppermute x10, starting transfers between devices, per_device(): lax.ppermute(keyvals, 'seq', plan.share[-off])  29.2 us
  transfers between devices with their start and end apart: 46, of which 12 were waited for; matrix products, arithmetic and copies ran while one was open for 11% of the time, Pallas kernels for 0%

profile of v1, /device:TPU:0, one launch (start us, length us, event | category | flops | bytes accessed | tf_op | source)
XLA Modules:
  0.0 756.6 jit_solution(6590006632114684503)
XLA Ops:
  17.0 8.3 %collective-permute-start.6 = (bf16[768,128]{0,1:T(8,128)(2,1)}, bf16[768,128]{0,1:T(8,128)(2,1)}, u32[]{:S(2)}, u32[]{:S(2)}) collective-permute-start(bf16[768,128]{0,1:T(8,128)(2,1)} %fusion.35), channel_id=1, source_target_pairs={{0,8},{2,10},{10,18},{12,20},{20,28},{22,30},{1,9},{3,11},{11,19},... | collective-permute-start | bytes 589832 | tf_op jit(solution)/shard_map/ppermute | solution.py:366
  25.3 4.8 collective-permute-start.5
  88.0 7.1 collective-permute-start.8
  100.8 4.6 collective-permute-start.21
  105.4 5.5 collective-permute-start.20
  120.0 9.2 %collective-permute-done.22 = bf16[128,768]{1,0:T(8,128)(2,1)S(1)} collective-permute-done((bf16[128,768]{1,0:T(8,128)(2,1)S(1)}, bf16[128,768]{1,0:T(8,128)(2,1)S(1)}, u32[]{:S(2)}, u32[]{:S(2)}) %collective-permute-start.22) | collective-permute-done | bytes 196640 | tf_op jit(solution)/shard_map/ppermute | solution.py:130
  135.4 6.4 collective-permute-done.10
  142.5 5.1 collective-permute-start.2
  150.9 5.8 collective-permute-start
  160.4 12.2 %collective-permute-done.3 = bf16[128,768]{1,0:T(8,128)(2,1)S(1)} collective-permute-done((bf16[128,768]{1,0:T(8,128)(2,1)S(1)}, bf16[128,768]{1,0:T(8,128)(2,1)S(1)}, u32[]{:S(2)}, u32[]{:S(2)}) %collective-permute-start.3) | collective-permute-done | bytes 196640 | tf_op jit(solution)/shard_map/ppermute | solution.py:130
  197.3 7.3 concatenate.72
  204.6 7.3 concatenate.74
  212.0 5.0 pad_maximum_fusion.k_ref
  219.2 27.4 %attend.1 = (bf16[768,768]{1,0:T(8,128)(2,1)}, f32[6,1,1536]{2,1,0:T(1,128)}) custom-call(s32[13]{0:T(128)} %pad_add_fusion.meta, bf16[768,768]{1,0:T(8,128)(2,1)} %get-tuple-element.118.q_ref, bf16[2,4480,256]{2,1,0:T(8,128)(2,1)} %pad_maximum_fusion.k_ref, bf16[2,80,4480]{2,1,0:T(8,128)(2,1)} %pad_maximum_fusion.2.vt_ref), custom_call_target="tpu_custom_call" | custom-call | tf_op jit(solution)/shard_map/attend/pallas_call | solution.py:417
  250.1 6.8 fusion.48
  257.0 11.8 %convolution_convert_fusion = bf16[3072,768]{1,0:T(8,128)(2,1)} fusion(bf16[768,768]{1,0:T(8,128)(2,1)S(1)} %copy-done.25, f32[768,3072]{1,0:T(8,128)} %fusion.48, f32[3072]{0:T(1024)S(1)} %copy-done.56), kind=kOutput, calls=%fused_computation.11 | convolution fusion | flops 3649830912 | bytes 15347712 | tf_op jit(solution)/shard_map/dot_general | solution.py:163
  268.8 12.1 %convert_reduce_fusion = (f32[3072]{0:T(1024)}, bf16[768,3072]{1,0:T(8,128)(2,1)S(1)}) fusion(f32[768,3072]{1,0:T(8,128)} %fusion.48, f32[3072]{0:T(1024)S(1)} %copy-done.56, bf16[768,768]{1,0:T(8,128)(2,1)S(1)} %copy-done.25, bf16[3072,768]{1,0:T(8,128)(2,1)S(1)} %bitcast.154), kind=kOutput, calls=%fused_computation.9 | convolution fusion | flops 3678139392 | bytes 20078592 | tf_op jit(solution)/shard_map/dot_general | solution.py:163
  280.9 4.8 multiply_reduce_fusion
  285.7 6.4 convolution_convert_fusion.1
  307.2 66.9 %attend_back.1 = (bf16[768,768]{1,0:T(8,128)(2,1)}, f32[2,128,4480]{2,1,0:T(8,128)}) custom-call(s32[13]{0:T(128)} %pad_add_fusion.meta, bf16[768,768]{1,0:T(8,128)(2,1)} %get-tuple-element.118.q_ref, bf16[768,768]{1,0:T(8,128)(2,1)} %fusion.34.g_ref, bf16[768,768]{1,0:T(8,128)(2,1)} %get-tuple-element.20.o_ref, f32[6,1,1536]{2,1,0:T(1,128)} %get-tuple-element.21.lse_ref, ...), custom_call_target="tpu_custom_call" | custom-call | tf_op jit(solution)/shard_map/attend_back/pallas_call | solution.py:462
  380.2 12.6 %constant_dynamic-update-slice_fusion.21 = (bf16[1408,768]{1,0:T(8,128)(2,1)}, bf16[768,768]{1,0:T(8,128)(2,1)}) fusion(f32[768]{0:T(1024)S(1)} %copy-done.60, f32[768,768]{1,0:T(8,128)S(1)} %copy-done.9, bf16[3072,768]{1,0:T(8,128)(2,1)} %param.63, f32[768,3072]{1,0:T(8,128)} %fusion.48, f32[3072]{0:T(1024)S(1)} %copy-done.57), kind=kOutput, calls=%fused_computation.158 | convolution fusion | flops 3649241088 | bytes 18889728 | tf_op jit(solution)/shard_map/dot_general | solution.py:163
  398.3 10.4 %dynamic_update_slice.6 = f32[8448,128]{0,1:T(8,128)} dynamic-update-slice(f32[8448,128]{0,1:T(8,128)} %broadcast_in_dim.74, f32[4096,128]{0,1:T(8,128)} %slice_bitcast_fusion.2, s32[]{:T(128)S(6)} %select_n.224, s32[]{:T(128)} %constant.130.clone.1) | dynamic-update-slice | bytes 4194308 | tf_op jit(solution)/shard_map/dynamic_update_slice | solution.py:494
  412.9 10.4 %dynamic_update_slice.7 = f32[8448,128]{0,1:T(8,128)} dynamic-update-slice(f32[8448,128]{0,1:T(8,128)} %dynamic_update_slice.6, f32[4096,128]{0,1:T(8,128)} %fusion.32, s32[]{:T(128)S(6)} %select_n.227, s32[]{:T(128)} %constant.130.clone.1) | dynamic-update-slice | bytes 4194308 | tf_op jit(solution)/shard_map/dynamic_update_slice | solution.py:494
  427.3 6.8 collective-permute-start.44
  436.8 8.4 %collective-permute-start.41 = (bf16[768,128]{0,1:T(8,128)(2,1)S(1)}, bf16[768,128]{0,1:T(8,128)(2,1)S(1)}, u32[]{:S(2)}, u32[]{:S(2)}) collective-permute-start(bf16[768,128]{0,1:T(8,128)(2,1)S(1)} %get-tuple-element.48), channel_id=1, source_target_pairs={{0,4},{2,6},{4,8},{6,10},{10,14},{12,16},{14,18},{16,20},{20,24},{... | collective-permute-start | bytes 589832 | tf_op jit(solution)/shard_map/ppermute | solution.py:500
  459.1 17.3 %collective-permute-start.18 = (bf16[128,768]{1,0:T(8,128)(2,1)}, bf16[128,768]{1,0:T(8,128)(2,1)}, u32[]{:S(2)}, u32[]{:S(2)}) collective-permute-start(bf16[128,768]{1,0:T(8,128)(2,1)} %get-tuple-element.73), channel_id=1, source_target_pairs={{10,4},{0,10},{14,12},{20,14},{12,20},{11,5},{1,11},{15,13},{21,15... | collective-permute-start | bytes 589832 | tf_op jit(solution)/shard_map/ppermute | solution.py:144
  479.6 4.6 collective-permute-start.30
  507.9 4.5 collective-permute-start.15
  526.4 50.2 %psum.42 = f32[8512]{0:T(1024)S(1)} all-reduce(f32[8512]{0:T(1024)S(1)} %concatenate.87), channel_id=1, replica_groups=mesh['seq'=16,'dp'=2] {'seq','dp'}, use_global_device_ids=true, to_apply=%region_23.24 | all-reduce | flops 8512 | bytes 68096 | tf_op jit(solution)/shard_map/psum | solution.py:528
  595.0 4.5 collective-permute-start.25
  614.6 118.8 %all-reduce.6.cloned.1.call-done = (bf16[768,768]{1,0:T(8,128)(2,1)}, bf16[768,128]{1,0:T(8,128)(2,1)}, bf16[768,768]{1,0:T(8,128)(2,1)}, bf16[768,3072]{1,0:T(8,128)(2,1)}, bf16[3072,768]{1,0:T(8,128)(2,1)}) async-done(((bf16[768,768]{1,0:T(8,128)(2,1)}, bf16[768,128]{1,0:T(8,128)(2,1)}, bf16[768,768]{1,0:T(8,128)(2,1)}, bf16[768,3072]{1,0:T(8,128)(2,1)}, bf16[3072,768]{1,0:T(8,128)(2,1)}), ...) | async-done | bytes 11993104 | tf_op jit(solution)/shard_map/psum | solution.py:530
  739.8 5.0 convert_element_type.198
  (387 shorter events, 237.4 us)
Async XLA Ops:
  7.2 726.2 %all-reduce.6.cloned.1.call-start = ((), (), s32[]{:S(2)}) async-start(), calls=%async_computation | async-start | bytes 23986176 | tf_op jit(solution)/shard_map/psum | solution.py:530
  13.1 144.5 %collective-permute-start.14 = (bf16[768,128]{0,1:T(8,128)(2,1)}, bf16[768,128]{0,1:T(8,128)(2,1)}, u32[]{:S(2)}, u32[]{:S(2)}) collective-permute-start(bf16[768,128]{0,1:T(8,128)(2,1)} %fusion.35), channel_id=1, source_target_pairs={{10,0},{20,10},{30,20},{11,1},{21,11},{31,21}} | collective-permute-start | bytes 589832 | tf_op jit(solution)/shard_map/ppermute | solution.py:366
  14.4 136.4 %collective-permute-start.13 = (bf16[768,128]{0,1:T(8,128)(2,1)}, bf16[768,128]{0,1:T(8,128)(2,1)}, u32[]{:S(2)}, u32[]{:S(2)}) collective-permute-start(bf16[768,128]{0,1:T(8,128)(2,1)} %fusion.35), channel_id=1, source_target_pairs={{8,0},{10,2},{18,10},{20,12},{28,20},{30,22},{9,1},{11,3},{19,11},... | collective-permute-start | bytes 589832 | tf_op jit(solution)/shard_map/ppermute | solution.py:366
  15.7 131.9 %collective-permute-start.12 = (bf16[768,128]{0,1:T(8,128)(2,1)}, bf16[768,128]{0,1:T(8,128)(2,1)}, u32[]{:S(2)}, u32[]{:S(2)}) collective-permute-start(bf16[768,128]{0,1:T(8,128)(2,1)} %fusion.35), channel_id=1, source_target_pairs={{6,0},{8,2},{10,4},{16,10},{18,12},{20,14},{26,20},{28,22},{30,24}... | collective-permute-start | bytes 589832 | tf_op jit(solution)/shard_map/ppermute | solution.py:366
  17.0 71.0 %collective-permute-start.6 = (bf16[768,128]{0,1:T(8,128)(2,1)}, bf16[768,128]{0,1:T(8,128)(2,1)}, u32[]{:S(2)}, u32[]{:S(2)}) collective-permute-start(bf16[768,128]{0,1:T(8,128)(2,1)} %fusion.35), channel_id=1, source_target_pairs={{0,8},{2,10},{10,18},{12,20},{20,28},{22,30},{1,9},{3,11},{11,19},... | collective-permute-start | bytes 589832 | tf_op jit(solution)/shard_map/ppermute | solution.py:366
  25.3 60.5 %collective-permute-start.5 = (bf16[768,128]{0,1:T(8,128)(2,1)}, bf16[768,128]{0,1:T(8,128)(2,1)}, u32[]{:S(2)}, u32[]{:S(2)}) collective-permute-start(bf16[768,128]{0,1:T(8,128)(2,1)} %fusion.35), channel_id=1, source_target_pairs={{0,10},{10,20},{20,30},{1,11},{11,21},{21,31}} | collective-permute-start | bytes 589832 | tf_op jit(solution)/shard_map/ppermute | solution.py:366
  88.0 12.7 %collective-permute-start.8 = (bf16[768,128]{0,1:T(8,128)(2,1)}, bf16[768,128]{0,1:T(8,128)(2,1)S(1)}, u32[]{:S(2)}, u32[]{:S(2)}) collective-permute-start(bf16[768,128]{0,1:T(8,128)(2,1)} %fusion.35), channel_id=1, source_target_pairs={{0,4},{2,6},{4,8},{6,10},{10,14},{12,16},{14,18},{16,20},{20,24},{... | collective-permute-start | bytes 589832 | tf_op jit(solution)/shard_map/ppermute | solution.py:366
  100.8 17.9 %collective-permute-start.21 = (bf16[128,768]{1,0:T(8,128)(2,1)S(1)}, bf16[128,768]{1,0:T(8,128)(2,1)S(1)}, u32[]{:S(2)}, u32[]{:S(2)}) collective-permute-start(bf16[128,768]{1,0:T(8,128)(2,1)S(1)} %get-tuple-element.69), channel_id=1, source_target_pairs={{0,8},{2,6},{6,4},{8,2},{10,12},{12,18},{14,16},{16,20},{18,14},{2... | collective-permute-start | bytes 589832 | tf_op jit(solution)/shard_map/ppermute | solution.py:130
  114.6 14.6 %collective-permute-start.22 = (bf16[128,768]{1,0:T(8,128)(2,1)S(1)}, bf16[128,768]{1,0:T(8,128)(2,1)S(1)}, u32[]{:S(2)}, u32[]{:S(2)}) collective-permute-start(bf16[128,768]{1,0:T(8,128)(2,1)S(1)} %get-tuple-element.68), channel_id=1, source_target_pairs={{0,8},{2,6},{4,10},{6,4},{8,2},{10,0},{12,18},{14,16},{16,20},{18,... | collective-permute-start | bytes 589832 | tf_op jit(solution)/shard_map/ppermute | solution.py:130
  118.7 14.0 %collective-permute-start.23 = (bf16[128,768]{1,0:T(8,128)(2,1)S(1)}, bf16[128,768]{1,0:T(8,128)(2,1)S(1)}, u32[]{:S(2)}, u32[]{:S(2)}) collective-permute-start(bf16[128,768]{1,0:T(8,128)(2,1)S(1)} %get-tuple-element.71), channel_id=1, source_target_pairs={{4,10},{10,0},{12,14},{14,20},{20,12},{5,11},{11,1},{13,15},{15,21... | collective-permute-start | bytes 589832 | tf_op jit(solution)/shard_map/ppermute | solution.py:130
  141.8 31.8 %collective-permute-start.4 = (bf16[128,768]{1,0:T(8,128)(2,1)S(1)}, bf16[128,768]{1,0:T(8,128)(2,1)S(1)}, u32[]{:S(2)}, u32[]{:S(2)}) collective-permute-start(bf16[128,768]{1,0:T(8,128)(2,1)S(1)} %get-tuple-element.77), channel_id=1, source_target_pairs={{10,12},{12,14},{14,20},{20,30},{11,13},{13,15},{15,21},{21,31}} | collective-permute-start | bytes 589832 | tf_op jit(solution)/shard_map/ppermute | solution.py:130
  142.5 17.9 %collective-permute-start.2 = (bf16[128,768]{1,0:T(8,128)(2,1)S(1)}, bf16[128,768]{1,0:T(8,128)(2,1)S(1)}, u32[]{:S(2)}, u32[]{:S(2)}) collective-permute-start(bf16[128,768]{1,0:T(8,128)(2,1)S(1)} %get-tuple-element.78), channel_id=1, source_target_pairs={{0,8},{2,6},{4,10},{6,4},{8,2},{10,0},{12,18},{14,16},{16,20},{18,... | collective-permute-start | bytes 589832 | tf_op jit(solution)/shard_map/ppermute | solution.py:130
  157.6 15.0 %collective-permute-start.3 = (bf16[128,768]{1,0:T(8,128)(2,1)S(1)}, bf16[128,768]{1,0:T(8,128)(2,1)S(1)}, u32[]{:S(2)}, u32[]{:S(2)}) collective-permute-start(bf16[128,768]{1,0:T(8,128)(2,1)S(1)} %get-tuple-element.81), channel_id=1, source_target_pairs={{4,10},{10,0},{12,14},{14,20},{20,12},{5,11},{11,1},{13,15},{15,21... | collective-permute-start | bytes 589832 | tf_op jit(solution)/shard_map/ppermute | solution.py:130
  425.9 22.5 %collective-permute-start.35 = (bf16[768,128]{0,1:T(8,128)(2,1)S(1)}, bf16[768,128]{0,1:T(8,128)(2,1)S(1)}, u32[]{:S(2)}, u32[]{:S(2)}) collective-permute-start(bf16[768,128]{0,1:T(8,128)(2,1)S(1)} %get-tuple-element.44), channel_id=1, source_target_pairs={{10,0},{20,10},{30,20},{11,1},{21,11},{31,21}} | collective-permute-start | bytes 589832 | tf_op jit(solution)/shard_map/ppermute | solution.py:500
  427.3 22.4 %collective-permute-start.44 = (bf16[768,128]{0,1:T(8,128)(2,1)S(1)}, bf16[768,128]{0,1:T(8,128)(2,1)S(1)}, u32[]{:S(2)}, u32[]{:S(2)}) collective-permute-start(bf16[768,128]{0,1:T(8,128)(2,1)S(1)} %get-tuple-element.45), channel_id=1, source_target_pairs={{0,10},{10,20},{20,30},{1,11},{11,21},{21,31}} | collective-permute-start | bytes 589832 | tf_op jit(solution)/shard_map/ppermute | solution.py:500
  434.1 16.9 %collective-permute-start.43 = (bf16[768,128]{0,1:T(8,128)(2,1)S(1)}, bf16[768,128]{0,1:T(8,128)(2,1)S(1)}, u32[]{:S(2)}, u32[]{:S(2)}) collective-permute-start(bf16[768,128]{0,1:T(8,128)(2,1)S(1)} %get-tuple-element.46), channel_id=1, source_target_pairs={{0,8},{2,10},{10,18},{12,20},{20,28},{22,30},{1,9},{3,11},{11,19},... | collective-permute-start | bytes 589832 | tf_op jit(solution)/shard_map/ppermute | solution.py:500
  435.4 16.9 %collective-permute-start.42 = (bf16[768,128]{0,1:T(8,128)(2,1)S(1)}, bf16[768,128]{0,1:T(8,128)(2,1)S(1)}, u32[]{:S(2)}, u32[]{:S(2)}) collective-permute-start(bf16[768,128]{0,1:T(8,128)(2,1)S(1)} %get-tuple-element.47), channel_id=1, source_target_pairs={{0,6},{2,8},{4,10},{10,16},{12,18},{14,20},{20,26},{22,28},{24,30}... | collective-permute-start | bytes 589832 | tf_op jit(solution)/shard_map/ppermute | solution.py:500
  436.8 17.9 %collective-permute-start.41 = (bf16[768,128]{0,1:T(8,128)(2,1)S(1)}, bf16[768,128]{0,1:T(8,128)(2,1)S(1)}, u32[]{:S(2)}, u32[]{:S(2)}) collective-permute-start(bf16[768,128]{0,1:T(8,128)(2,1)S(1)} %get-tuple-element.48), channel_id=1, source_target_pairs={{0,4},{2,6},{4,8},{6,10},{10,14},{12,16},{14,18},{16,20},{20,24},{... | collective-permute-start | bytes 589832 | tf_op jit(solution)/shard_map/ppermute | solution.py:500
  451.0 25.4 %collective-permute-start.38 = (bf16[768,128]{0,1:T(8,128)(2,1)S(1)}, bf16[768,128]{0,1:T(8,128)(2,1)S(1)}, u32[]{:S(2)}, u32[]{:S(2)}) collective-permute-start(bf16[768,128]{0,1:T(8,128)(2,1)S(1)} %get-tuple-element.51), channel_id=1, source_target_pairs={{4,0},{6,2},{8,4},{10,6},{14,10},{16,12},{18,14},{20,16},{24,20},{... | collective-permute-start | bytes 589832 | tf_op jit(solution)/shard_map/ppermute | solution.py:500
  452.3 26.0 %collective-permute-start.37 = (bf16[768,128]{0,1:T(8,128)(2,1)S(1)}, bf16[768,128]{0,1:T(8,128)(2,1)S(1)}, u32[]{:S(2)}, u32[]{:S(2)}) collective-permute-start(bf16[768,128]{0,1:T(8,128)(2,1)S(1)} %get-tuple-element.52), channel_id=1, source_target_pairs={{6,0},{8,2},{10,4},{16,10},{18,12},{20,14},{26,20},{28,22},{30,24}... | collective-permute-start | bytes 589832 | tf_op jit(solution)/shard_map/ppermute | solution.py:500
  454.7 24.9 %collective-permute-start.36 = (bf16[768,128]{0,1:T(8,128)(2,1)S(1)}, bf16[768,128]{0,1:T(8,128)(2,1)S(1)}, u32[]{:S(2)}, u32[]{:S(2)}) collective-permute-start(bf16[768,128]{0,1:T(8,128)(2,1)S(1)} %get-tuple-element.53), channel_id=1, source_target_pairs={{8,0},{10,2},{18,10},{20,12},{28,20},{30,22},{9,1},{11,3},{19,11},... | collective-permute-start | bytes 589832 | tf_op jit(solution)/shard_map/ppermute | solution.py:500
  457.7 137.2 %collective-permute-start.19 = (bf16[128,768]{1,0:T(8,128)(2,1)}, bf16[128,768]{1,0:T(8,128)(2,1)}, u32[]{:S(2)}, u32[]{:S(2)}) collective-permute-start(bf16[128,768]{1,0:T(8,128)(2,1)} %get-tuple-element.72), channel_id=1, source_target_pairs={{12,10},{14,12},{20,14},{30,20},{13,11},{15,13},{21,15},{31,21}} | collective-permute-start | bytes 589832 | tf_op jit(solution)/shard_map/ppermute | solution.py:144
  459.1 133.0 %collective-permute-start.18 = (bf16[128,768]{1,0:T(8,128)(2,1)}, bf16[128,768]{1,0:T(8,128)(2,1)}, u32[]{:S(2)}, u32[]{:S(2)}) collective-permute-start(bf16[128,768]{1,0:T(8,128)(2,1)} %get-tuple-element.73), channel_id=1, source_target_pairs={{10,4},{0,10},{14,12},{20,14},{12,20},{11,5},{1,11},{15,13},{21,15... | collective-permute-start | bytes 589832 | tf_op jit(solution)/shard_map/ppermute | solution.py:144
  476.4 109.7 %collective-permute-start.17 = (bf16[128,768]{1,0:T(8,128)(2,1)}, bf16[128,768]{1,0:T(8,128)(2,1)}, u32[]{:S(2)}, u32[]{:S(2)}) collective-permute-start(bf16[128,768]{1,0:T(8,128)(2,1)} %get-tuple-element.74), channel_id=1, source_target_pairs={{8,0},{6,2},{10,4},{4,6},{2,8},{0,10},{18,12},{16,14},{20,16},{14,... | collective-permute-start | bytes 589832 | tf_op jit(solution)/shard_map/ppermute | solution.py:144
  478.3 15.9 %collective-permute-start.31 = (bf16[128,768]{0,1:T(8,128)(2,1)}, bf16[128,768]{0,1:T(8,128)(2,1)}, u32[]{:S(2)}, u32[]{:S(2)}) collective-permute-start(bf16[128,768]{0,1:T(8,128)(2,1)} %get-tuple-element.60), channel_id=1, source_target_pairs={{8,0},{6,2},{4,6},{2,8},{12,10},{18,12},{16,14},{20,16},{14,18},{1... | collective-permute-start | bytes 589832 | tf_op jit(solution)/shard_map/ppermute | solution.py:144
  505.8 74.5 %collective-permute-start.16 = (bf16[128,768]{1,0:T(8,128)(2,1)}, bf16[128,768]{1,0:T(8,128)(2,1)}, u32[]{:S(2)}, u32[]{:S(2)}) collective-permute-start(bf16[128,768]{1,0:T(8,128)(2,1)} %get-tuple-element.75), channel_id=1, source_target_pairs={{8,0},{6,2},{4,6},{2,8},{12,10},{18,12},{16,14},{20,16},{14,18},{1... | collective-permute-start | bytes 589832 | tf_op jit(solution)/shard_map/ppermute | solution.py:144
  507.9 70.0 %collective-permute-start.15 = (bf16[128,768]{1,0:T(8,128)(2,1)}, bf16[128,768]{1,0:T(8,128)(2,1)}, u32[]{:S(2)}, u32[]{:S(2)}) collective-permute-start(bf16[128,768]{1,0:T(8,128)(2,1)} %get-tuple-element.76), channel_id=1, source_target_pairs={{8,0},{6,2},{2,6},{0,8},{18,12},{16,14},{14,16},{12,18},{10,20},{2... | collective-permute-start | bytes 589832 | tf_op jit(solution)/shard_map/ppermute | solution.py:144
  577.9 33.1 %collective-permute-start.29 = (bf16[128,768]{1,0:T(8,128)(2,1)S(1)}, bf16[128,768]{1,0:T(8,128)(2,1)S(1)}, u32[]{:S(2)}, u32[]{:S(2)}) collective-permute-start(bf16[128,768]{1,0:T(8,128)(2,1)S(1)} %copy-done.31), channel_id=1, source_target_pairs={{12,10},{14,12},{20,14},{30,20},{13,11},{15,13},{21,15},{31,21}} | collective-permute-start | bytes 589832 | tf_op jit(solution)/shard_map/ppermute | solution.py:144
  580.4 30.6 %collective-permute-start.28 = (bf16[128,768]{1,0:T(8,128)(2,1)S(1)}, bf16[128,768]{1,0:T(8,128)(2,1)S(1)}, u32[]{:S(2)}, u32[]{:S(2)}) collective-permute-start(bf16[128,768]{1,0:T(8,128)(2,1)S(1)} %copy-done.32), channel_id=1, source_target_pairs={{10,4},{0,10},{14,12},{20,14},{12,20},{11,5},{1,11},{15,13},{21,15... | collective-permute-start | bytes 589832 | tf_op jit(solution)/shard_map/ppermute | solution.py:144
  586.1 24.8 %collective-permute-start.27 = (bf16[128,768]{1,0:T(8,128)(2,1)S(1)}, bf16[128,768]{1,0:T(8,128)(2,1)S(1)}, u32[]{:S(2)}, u32[]{:S(2)}) collective-permute-start(bf16[128,768]{1,0:T(8,128)(2,1)S(1)} %copy-done.33), channel_id=1, source_target_pairs={{8,0},{6,2},{10,4},{4,6},{2,8},{0,10},{18,12},{16,14},{20,16},{14,... | collective-permute-start | bytes 589832 | tf_op jit(solution)/shard_map/ppermute | solution.py:144
  592.1 18.8 %collective-permute-start.26 = (bf16[128,768]{1,0:T(8,128)(2,1)S(1)}, bf16[128,768]{1,0:T(8,128)(2,1)S(1)}, u32[]{:S(2)}, u32[]{:S(2)}) collective-permute-start(bf16[128,768]{1,0:T(8,128)(2,1)S(1)} %copy-done.34), channel_id=1, source_target_pairs={{8,0},{6,2},{4,6},{2,8},{12,10},{18,12},{16,14},{20,16},{14,18},{1... | collective-permute-start | bytes 589832 | tf_op jit(solution)/shard_map/ppermute | solution.py:144
  595.0 15.9 %collective-permute-start.25 = (bf16[128,768]{1,0:T(8,128)(2,1)S(1)}, bf16[128,768]{1,0:T(8,128)(2,1)S(1)}, u32[]{:S(2)}, u32[]{:S(2)}) collective-permute-start(bf16[128,768]{1,0:T(8,128)(2,1)S(1)} %copy-done.35), channel_id=1, source_target_pairs={{8,0},{6,2},{2,6},{0,8},{18,12},{16,14},{14,16},{12,18},{10,20},{2... | collective-permute-start | bytes 589832 | tf_op jit(solution)/shard_map/ppermute | solution.py:144
  (84 other events, 1390.6 us)
Sparse Core Ops, SparseCore 0:
  486.5 246.9 all-reduce.5

commit v2 on v0

v2 whole, which is shorter than its diff:
```python
from functools import partial

import jax
import jax.numpy as jnp
import numpy as np
from jax import lax
from jax.experimental import pallas as pl
from jax.experimental.pallas import tpu as pltpu
from jax.sharding import PartitionSpec as P

ROW = 4096
CHUNK = 128
BLOCK = 512
PAD = BLOCK - CHUNK
LOG2E = 1.4426950408889634
BIG = -1e30
MARGIN = BLOCK
PIECE = 1024
DELAYS = (2, 8, 4, 3, 3, 2, 3, 5, 8, 3)
SAFE = 60.0
epsilon = 1e-05
GELU = 0.7978845608028654
bf16 = jnp.bfloat16
f32 = jnp.float32


class Plan:
    def __init__(self, devices, shard_len):
        self.devices = devices
        self.shard_len = shard_len
        self.per_dev = shard_len // CHUNK
        self.per_row = ROW // CHUNK
        assert shard_len % CHUNK == 0 and shard_len <= ROW
        ends = [(d + 1) * shard_len - self.first_row(d) * ROW for d in range(devices)]
        self.span = -(-max(ends) // BLOCK) * BLOCK
        self.window = MARGIN + self.span
        self.reach = max(
            d - e for d in range(devices) for e in range(d + 1) if self.first_row(d) <= self.last_row(e)
        )

    def first_row(self, device):
        return device * self.shard_len // ROW

    def last_row(self, device):
        return ((device + 1) * self.shard_len - 1) // ROW

    def feeds(self, source, holder):
        return (
            (source >= 0) & (holder < self.devices) & (self.first_row(holder) <= self.last_row(source))
        )

    def place(self, source, holder):
        return MARGIN + source * self.shard_len - self.first_row(holder) * ROW

    def chunk(self, device, i):
        return device * self.per_dev + i - self.first_row(device) * self.per_row


class Summing:
    def __init__(self, plan, pieces, height, mat, inbox, extra, sems):
        self.pieces, self.height = pieces, height
        self.mat, self.inbox, self.extra = mat, inbox, extra
        self.out_send, self.out_recv, self.back_send, self.back_recv, self.free = sems
        self.bits = plan.devices.bit_length() - 1
        self.halvings = 1 + min(self.bits, 4)
        self.swaps = self.bits + 1 - self.halvings
        self.stages = 2 * self.halvings + self.swaps
        self.seq, self.dp = lax.axis_index("seq"), lax.axis_index("dp")

    @staticmethod
    def scratch(plan, pieces, height, width):
        bits = plan.devices.bit_length() - 1
        halvings = 1 + min(bits, 4)
        swaps = bits + 1 - halvings
        last = height >> halvings
        dma = pltpu.SemaphoreType.DMA
        return [
            pltpu.VMEM((pieces, height - last, width), bf16),
            pltpu.VMEM((max(swaps, 1), pieces, last, width), bf16),
            dma((halvings + swaps, pieces)),
            dma((halvings + swaps, pieces)),
            dma((halvings, pieces)),
            dma((halvings, pieces)),
            pltpu.SemaphoreType.REGULAR((halvings, pieces)),
        ]

    def partners(self):
        bits = [(self.seq >> b) & 1 for b in range(self.bits)]
        return [(self.seq, 1 - self.dp)] + [
            (self.seq + (1 - 2 * bit) * (1 << b), self.dp) for b, bit in enumerate(bits)
        ]

    def turn(self, t, p):
        if t == 0:
            return self.dp, {"seq": self.seq, "dp": 1 - self.dp}
        if t < 4:
            b = (p + (t - 1)) % 3
            step = jnp.where(b == 0, 1, jnp.where(b == 1, 2, 4))
        else:
            step = 1 << (t - 1)
        bit = (self.seq // step) % 2
        return bit, {"seq": self.seq + (1 - 2 * bit) * step, "dp": self.dp}

    def base(self, t, p):
        at = 0
        for u in range(t):
            bit, _ = self.turn(u, p)
            at = at + bit * (self.height >> (u + 1))
        return at

    def rows(self, start, size):
        return pl.ds(pl.multiple_of(start, size), size)

    def copy(self, stage, p):
        h, w = self.halvings, self.swaps
        if stage < h:
            t, size = stage, self.height >> (stage + 1)
            bit, device = self.turn(t, p)
            src = self.mat.at[p, self.rows(self.base(t, p) + (1 - bit) * size, size)]
            dst = self.inbox.at[p, pl.ds(self.height - 2 * size, size)]
            sems = self.out_send.at[t, p], self.out_recv.at[t, p]
        elif stage < h + w:
            t, size = stage, self.height >> h
            _, device = self.turn(t, p)
            src = self.mat.at[p, self.rows(self.base(h, p), size)]
            dst = self.extra.at[t - h, p]
            sems = self.out_send.at[t, p], self.out_recv.at[t, p]
        else:
            t = self.stages - 1 - stage
            size = self.height >> (t + 1)
            _, device = self.turn(t, p)
            src = self.mat.at[p, self.rows(self.base(t + 1, p), size)]
            dst = src
            sems = self.back_send.at[t, p], self.back_recv.at[t, p]
        return pltpu.make_async_remote_copy(
            src_ref=src,
            dst_ref=dst,
            send_sem=sems[0],
            recv_sem=sems[1],
            device_id=device,
            device_id_type=pl.DeviceIdType.MESH,
        )

    def event(self, stage, p):
        if stage > 0:
            before = stage - 1
            self.copy(before, p).wait()
            h = self.halvings
            if before < h:
                size = self.height >> (before + 1)
                at = self.rows(self.base(before + 1, p), size)
                self.mat[p, at, :] = self.mat[p, at, :] + self.inbox[p, pl.ds(self.height - 2 * size, size), :]
                _, device = self.turn(before, p)
                pl.semaphore_signal(
                    self.free.at[before, p], inc=1, device_id=device, device_id_type=pl.DeviceIdType.MESH
                )
            elif before < h + self.swaps:
                at = self.rows(self.base(h, p), self.height >> h)
                self.mat[p, at, :] = self.mat[p, at, :] + self.extra[before - h, p]
        if stage >= self.halvings + self.swaps and stage < self.stages:
            pl.semaphore_wait(self.free.at[self.stages - 1 - stage, p], 1)
        if stage < self.stages:
            self.copy(stage, p).start()

    def step(self, n, starts, first=None, last=None):
        for stage in range(self.stages, -1, -1):
            p = n - starts[stage]

            @pl.when((p >= 0) & (p < self.pieces))
            def _():
                if stage == 0 and first is not None:
                    first(p)
                self.event(stage, p)
                if stage == self.stages and last is not None:
                    last(p)

    def starts(self, delays):
        h = self.halvings
        full = [delays[s] for s in range(h)] + [delays[h - 1]] * self.swaps + list(delays[5 : 5 + h])
        at = [0]
        for d in full:
            at.append(at[-1] + d)
        return at


def line(ref):
    return ref[...].reshape(1, ref.shape[0])


def remote(src, dst, send, recv, device):
    return pltpu.make_async_remote_copy(
        src_ref=src,
        dst_ref=dst,
        send_sem=send,
        recv_sem=recv,
        device_id={"seq": device},
        device_id_type=pl.DeviceIdType.MESH,
    )


def greet(plan, me, others=()):
    barrier = pltpu.get_barrier_semaphore()
    count = len(others)
    for seq, dp in others:
        pl.semaphore_signal(
            barrier, inc=1, device_id={"seq": seq, "dp": dp}, device_id_type=pl.DeviceIdType.MESH
        )
    for off in range(1, plan.reach + 1):
        for there, device in ((plan.feeds(me, me + off), me + off), (plan.feeds(me - off, me), me - off)):
            count = count + jnp.where(there, 1, 0)

            @pl.when(there)
            def _():
                pl.semaphore_signal(
                    barrier, inc=1, device_id={"seq": device}, device_id_type=pl.DeviceIdType.MESH
                )

    pl.semaphore_wait(barrier, count)


def gather_kernel(
    plan,
    tok_ref, gain_ref, shift_ref, wkv_ref, kvb_ref, wq_ref, qb_ref,
    normal_ref, q_ref, win_ref,
    kv_ref, kv_send, kv_recv,
):
    me = lax.axis_index("seq")
    greet(plan, me)

    def copy(off, source, holder):
        at = pl.multiple_of(plan.place(source, holder), CHUNK)
        return remote(
            kv_ref, win_ref.at[pl.ds(at, plan.shard_len)], kv_send.at[off - 1], kv_recv.at[off - 1], holder
        )

    normal = normed(tok_ref[...].astype(f32), line(gain_ref), line(shift_ref)).astype(bf16)
    normal_ref[...] = normal
    bias = line(kvb_ref)
    bias = jnp.concatenate([jnp.zeros_like(bias), bias], axis=1)
    kv_ref[...] = (contract(normal, wkv_ref[...], 1, 0) + bias).astype(bf16)
    for off in range(1, plan.reach + 1):

        @pl.when(plan.feeds(me, me + off))
        def _():
            copy(off, me, me + off).start()

    own = pl.multiple_of(plan.place(me, me), CHUNK)
    win_ref[pl.ds(own, plan.shard_len), :] = kv_ref[...]
    q_ref[...] = (contract(normal, wq_ref[...], 1, 0) + line(qb_ref)).T.astype(bf16)
    for off in range(1, plan.reach + 1):

        @pl.when(plan.feeds(me, me + off))
        def _():
            copy(off, me, me + off).wait_send()

        @pl.when(plan.feeds(me - off, me))
        def _():
            at = pl.multiple_of(plan.place(me - off, me), CHUNK)
            remote(
                kv_ref, win_ref.at[pl.ds(at, plan.shard_len)], kv_send.at[off - 1], kv_recv.at[off - 1], me - off
            ).wait_recv()


def normed(values, gains, shifts):
    center = values - jnp.mean(values, axis=-1, keepdims=True)
    spread = jnp.mean(center * center, axis=-1, keepdims=True)
    return center * lax.rsqrt(spread + epsilon) * gains + shifts


def contract(left_op, right_op, left_dim, right_dim):
    return lax.dot_general(
        left_op, right_op, (((left_dim,), (right_dim,)), ((), ())), preferred_element_type=f32
    )


def wide(block, heads, head_dim):
    return jnp.concatenate([block[h * head_dim : (h + 1) * head_dim] for h in range(heads)], axis=1)


def tall(block, heads):
    return jnp.concatenate([block[:, h * CHUNK : (h + 1) * CHUNK] for h in range(heads)], axis=0)


def hi_lo(value, count):
    parts = []
    for _ in range(count):
        part = value.astype(bf16)
        parts.append(part.astype(f32))
        value = value - parts[-1]
    return parts


def scaled_queries(q, head_dim, lse_parts, row):
    width = q.shape[1]
    hi, lo = hi_lo(q.astype(f32) * (LOG2E * head_dim ** (-0.5)), 2)
    first = jnp.broadcast_to(jnp.where(row == 0, 1.0, 0.0), (1, width))
    fill = jnp.zeros((2 * head_dim - 5, width), f32)
    return jnp.concatenate([hi, lo] + lse_parts + [first, 1.0 - first, fill], axis=0).astype(bf16)


def triangle(heads):
    key = lax.broadcasted_iota(jnp.int32, (CHUNK, heads * CHUNK), 0)
    query = lax.broadcasted_iota(jnp.int32, (CHUNK, heads * CHUNK), 1) % CHUNK
    return key <= query


def causal(s, heads):
    return jnp.concatenate([s[:PAD], jnp.where(triangle(heads), s[PAD:], BIG)], axis=0)


def attend_kernel(
    plan, heads, head_dim, len_ref, q_ref, win_ref, o_ref, rest_ref, lse_ref, k_ref, v_ref, kt_ref, vt_ref, acc, top, norm
):
    i = pl.program_id(0)
    me = lax.axis_index("seq")
    place = plan.chunk(me, i)
    row = place // (ROW // CHUNK)
    end = MARGIN + (place + 1) * CHUNK
    blocks = place % (ROW // CHUNK) // (BLOCK // CHUNK) + 1

    @pl.when(i == 0)
    def _():
        first, second = len_ref[0, plan.first_row(me)], len_ref[0, plan.last_row(me)]
        filled = plan.place(me, me) + plan.shard_len - MARGIN
        lane = lax.broadcasted_iota(jnp.int32, (BLOCK, 2 * head_dim), 1)
        vt_ref[head_dim:, :] = jnp.where(
            lax.broadcasted_iota(jnp.int32, (16, vt_ref.shape[1]), 0) == 0, 1.0, 0.0
        ).astype(bf16)
        norm[...] = jnp.zeros_like(norm)

        def fill(b, _):
            at = pl.ds(pl.multiple_of(b * BLOCK, BLOCK), BLOCK)
            pos = b * BLOCK - MARGIN + lax.broadcasted_iota(jnp.int32, (BLOCK, 2 * head_dim), 0)
            inside = (pos >= 0) & (pos < filled)
            both = jnp.where(inside, win_ref[at, :].astype(f32), 0.0)
            swapped = pltpu.roll(both, head_dim, 1)
            k_ref[at, : 2 * head_dim] = jnp.where(lane < head_dim, both, swapped).astype(bf16)
            one = (pos >= 0) & (pos < first)
            two = (pos >= ROW) & (pos < ROW + second)
            bias = jnp.where(lane == 3, jnp.where(one, 0.0, BIG), jnp.where(two, 0.0, BIG))
            marks = jnp.where(lane < 3, 1.0, jnp.where(lane < 5, bias, 0.0))
            k_ref[at, 2 * head_dim :] = marks.astype(bf16)
            v_ref[at, :] = jnp.where(
                lane >= head_dim, both, jnp.where(lane < 3, 1.0, 0.0)
            ).astype(bf16)
            turned = both.T
            kt_ref[:, at] = turned[:head_dim].astype(bf16)
            vt_ref[:head_dim, at] = turned[head_dim:].astype(bf16)
            norm[...] = jnp.maximum(
                norm[...],
                jnp.max(jnp.sum(jnp.square(turned[:head_dim]), axis=0, keepdims=True), axis=1, keepdims=True),
            )
            return 0

        lax.fori_loop(0, k_ref.shape[0] // BLOCK, fill, 0)

    zero = jnp.zeros((1, heads * CHUNK), f32)
    q = wide(q_ref[...], heads, head_dim)
    q_aug = scaled_queries(q, head_dim, [zero, zero, zero], row)
    q_norm = jnp.max(jnp.sum(jnp.square(q.astype(f32)), axis=0, keepdims=True), axis=1, keepdims=True)
    limit = (SAFE / LOG2E) ** 2 * head_dim
    safe = jnp.max(jnp.where(q_norm * norm[...] < limit, 1, 0)) > 0

    def scores(j):
        off = pl.multiple_of(end - (j + 1) * BLOCK, CHUNK)
        return contract(k_ref[pl.ds(off, BLOCK), :], q_aug, 1, 0)

    def values(j):
        off = pl.multiple_of(end - (j + 1) * BLOCK, CHUNK)
        return vt_ref[:, pl.ds(off, BLOCK)]

    @pl.when(safe)
    def _():
        p = jnp.exp2(causal(scores(0), heads)).astype(bf16)
        acc[...] = contract(values(0), p, 1, 0)

        def step(j, _):
            p = jnp.exp2(scores(j)).astype(bf16)
            acc[...] += contract(values(j), p, 1, 0)
            return 0

        lax.fori_loop(1, blocks, step, 0)
        top[...] = jnp.zeros_like(top)

    @pl.when(jnp.logical_not(safe))
    def _():
        s = causal(scores(0), heads)
        m = jnp.max(s, axis=0, keepdims=True)
        top[...] = m
        acc[...] = contract(values(0), jnp.exp2(s - m).astype(bf16), 1, 0)

        def step(j, _):
            s = scores(j)
            old = top[...]
            m = jnp.maximum(old, jnp.max(s, axis=0, keepdims=True))
            top[...] = m
            p = jnp.exp2(s - m).astype(bf16)
            acc[...] = acc[...] * jnp.exp2(old - m) + contract(values(j), p, 1, 0)
            return 0

        lax.fori_loop(1, blocks, step, 0)

    total = acc[head_dim : head_dim + 1, :]
    attended = tall(acc[:head_dim, :] / total, heads)
    o_ref[...] = attended.astype(bf16)
    rest_ref[...] = (attended - attended.astype(bf16).astype(f32)).astype(bf16)
    lse_ref[0] = top[...] + jnp.log2(total)


def feed_phase(
    att_ref, wo_hbm, tok_ref, cot_hbm, vecs, upb_ref, up_hbm, down_hbm,
    out_hbm, res_ref, gatt_ref, mat,
    up_buf, down_buf, normal, out_acc, gn_acc, wo_ref, cot_ref, out_ref, fetch, piece_done,
):
    tile = mat.shape[1] // 2
    tiles = up_hbm.shape[1] // tile
    width = up_hbm.shape[0]
    out_bias, gain, shift, down_bias = (line(ref) for ref in vecs)

    def fetches(t, slot):
        at = pl.ds(pl.multiple_of(t * tile, tile), tile)
        return (
            pltpu.make_async_copy(up_hbm.at[:, at], up_buf.at[slot], fetch.at[0, slot]),
            pltpu.make_async_copy(down_hbm.at[at], down_buf.at[slot], fetch.at[1, slot]),
        )

    wo_copy = pltpu.make_async_copy(wo_hbm, wo_ref, fetch.at[2, 0])
    cot_copy = pltpu.make_async_copy(cot_hbm, cot_ref, fetch.at[2, 1])
    wo_copy.start()
    for copy in fetches(0, 0):
        copy.start()
    cot_copy.start()
    wo_copy.wait()

    residual = tok_ref[...].astype(f32) + contract(att_ref[...], wo_ref[...], 0, 0) + out_bias
    res_ref[...] = residual
    normal[...] = normed(residual, gain, shift).astype(bf16)
    out_acc[...] = residual + down_bias
    gn_acc[...] = jnp.zeros_like(gn_acc)
    sums = mat.shape[0] - 1
    cot_copy.wait()

    def step(t, _):
        slot = t % 2
        for copy in fetches(t, slot):
            copy.wait()

        @pl.when(t + 1 < tiles)
        def _():
            for copy in fetches(t + 1, 1 - slot):
                copy.start()

        u = contract(normal[...], up_buf[slot], 1, 0) + upb_ref[t]
        square = u * u
        th = jnp.tanh(GELU * (u + 0.044715 * (u * square)))
        half = 0.5 * (1.0 + th)
        slope = half + (0.5 * GELU) * u * (1.0 - th * th) * (1.0 + 3 * 0.044715 * square)
        activated = (u * half).astype(bf16)
        out_acc[...] += contract(activated, down_buf[slot], 1, 0)
        mat[t, tile:, :] = contract(activated, cot_ref[...], 0, 0).astype(bf16)
        grad = (contract(cot_ref[...], down_buf[slot], 1, 1) * slope).astype(bf16)
        gn_acc[...] += contract(grad, up_buf[slot], 1, 1)
        mat[t, :tile, :] = contract(grad, normal[...], 0, 0).astype(bf16)
        upb_ref[t] = jnp.sum(grad.astype(f32), axis=0, keepdims=True)
        piece_done(t)
        return 0

    lax.fori_loop(0, tiles, step, 0)
    out_ref[...] = out_acc[...].astype(bf16)
    out_copy = pltpu.make_async_copy(out_ref, out_hbm, fetch.at[2, 0])
    out_copy.start()

    residual = res_ref[...]
    center = residual - jnp.mean(residual, axis=-1, keepdims=True)
    scale = lax.rsqrt(jnp.mean(center * center, axis=-1, keepdims=True) + epsilon)
    xhat = center * scale
    gn = gn_acc[...]
    q = gn * gain
    grad = scale * (
        q - jnp.mean(q, axis=-1, keepdims=True) - xhat * jnp.mean(q * xhat, axis=-1, keepdims=True)
    )
    cot = cot_ref[...].astype(f32)
    grad = cot + grad
    res_ref[...] = grad
    proj = grad.astype(bf16)
    mat[sums, :width, :] = contract(att_ref[...], proj, 1, 0).astype(bf16)
    rows = [cot, proj.astype(f32), gn * xhat, gn]
    rows = [jnp.sum(row, axis=0, keepdims=True) for row in rows]
    rows.append(jnp.zeros((16 - len(rows), width), f32))
    mat[sums, width : width + 16, :] = jnp.concatenate(rows, axis=0).astype(bf16)
    rows = [upb_ref[t] for t in range(tiles)] + [jnp.zeros((1, tile), f32)] * (16 - tiles)
    rows = jnp.concatenate([jnp.concatenate(rows, axis=0), jnp.zeros((16, width - tile), f32)], axis=1)
    mat[sums, width + 16 : width + 32, :] = rows.astype(bf16)
    rest = mat.shape[1] - width - 32
    mat[sums, width + 32 :, :] = jnp.zeros((rest, width), bf16)
    gatt_ref[...] = contract(wo_ref[...], proj, 1, 1).astype(bf16)
    out_copy.wait()


def back_phase(
    plan, heads, head_dim, me, talk, steps,
    q_hbm, k_hbm, v_hbm, kt_hbm, lse_ref, o_ref, rest_hbm, gatt_ref, dq_ref,
    low, inbox, kv_send, kv_recv,
    k_ref, v_ref, kt_ref, q_ref, q_mat, q_aug, g_aug, acc, total, rest_ref, fetch, prepared,
):
    shard_len = plan.shard_len
    copies = [
        pltpu.make_async_copy(src, dst, fetch.at[k])
        for k, (src, dst) in enumerate(
            [(q_hbm, q_ref), (rest_hbm, rest_ref), (k_hbm, k_ref), (v_hbm, v_ref), (kt_hbm, kt_ref)]
        )
    ]
    for copy in copies:
        copy.start()
    total[...] = jnp.zeros_like(total)
    acc[...] = jnp.zeros_like(acc)
    for copy in copies[:2]:
        copy.wait()
    for i in range(plan.per_dev):
        at = pl.ds(i * CHUNK, CHUNK)
        q = wide(q_ref[:, at], heads, head_dim)
        q_mat[i] = q
        row = plan.chunk(me, i) // plan.per_row
        q_aug[i] = scaled_queries(q, head_dim, hi_lo(-lse_ref[i], 3), row)
        g = wide(gatt_ref[:, at], heads, head_dim)
        o = wide(o_ref[:, at], heads, head_dim).astype(f32) + wide(rest_ref[:, at], heads, head_dim).astype(f32)
        delta = jnp.sum(g.astype(f32) * o, axis=0, keepdims=True)
        fill = jnp.zeros((head_dim - 3, heads * CHUNK), f32)
        marks = jnp.concatenate(hi_lo(-delta, 3) + [fill], axis=0).astype(bf16)
        g_aug[i] = jnp.concatenate([marks, g], axis=0)
    prepared()
    for copy in copies[2:]:
        copy.wait()

    def piece(off, source, holder):
        at = pl.ds(pl.multiple_of(plan.place(source, holder), CHUNK), shard_len)
        return remote(low.at[:, at], inbox.at[off - 1], kv_send.at[off - 1], kv_recv.at[off - 1], source)

    def block(i, at, place, diagonal):
        s = contract(k_ref[at, :], q_aug[i], 1, 0)
        if diagonal:
            key = lax.broadcasted_iota(jnp.int32, (BLOCK, heads * CHUNK), 0)
            query = lax.broadcasted_iota(jnp.int32, (BLOCK, heads * CHUNK), 1) % CHUNK
            s = jnp.where(key - query <= place % (BLOCK // CHUNK) * CHUNK, s, BIG)
        dp = contract(v_ref[at, :], g_aug[i], 1, 0)
        p = jnp.exp2(s)
        ds = (p * dp).astype(bf16)
        p = p.astype(bf16)
        acc[i] += contract(kt_ref[:, at], ds, 1, 0)
        total[:head_dim, at] += contract(q_mat[i], ds, 1, 1)
        total[head_dim:, at] += contract(g_aug[i, head_dim:, :], p, 1, 1)

    def key_step(b, n):
        at = pl.ds(pl.multiple_of(MARGIN + b * BLOCK, BLOCK), BLOCK)

        def chunk_step(i, n):
            place = plan.chunk(me, i)
            last = place // (BLOCK // CHUNK)
            active = (b <= last) & (b // (ROW // BLOCK) == place // plan.per_row)

            @pl.when(active)
            def _():
                talk(n)

            @pl.when(active & (b < last))
            def _():
                block(i, at, place, False)

            @pl.when(b == last)
            def _():
                block(i, at, place, True)

            return n + jnp.where(active, 1, 0)

        n = lax.fori_loop(0, plan.per_dev, chunk_step, n)
        for off in range(1, plan.reach + 1):
            end = plan.place(me - off, me) + shard_len - MARGIN

            @pl.when(plan.feeds(me - off, me) & (b == (end + BLOCK - 1) // BLOCK - 1))
            def _():
                at = pl.ds(pl.multiple_of(plan.place(me - off, me), CHUNK), shard_len)
                low[:head_dim, at] = (total[:head_dim, at] * head_dim ** (-0.5)).astype(bf16)
                low[head_dim:, at] = total[head_dim:, at].astype(bf16)
                piece(off, me - off, me).start()

        return n

    done = lax.fori_loop(0, plan.span // BLOCK, key_step, steps)
    for i in range(plan.per_dev):
        dq_ref[:, i * CHUNK : (i + 1) * CHUNK] = tall(acc[i] * head_dim ** (-0.5), heads).astype(bf16)
    own = pl.ds(pl.multiple_of(plan.place(me, me), CHUNK), shard_len)
    acc_kv = total[:, own]
    total[:, :shard_len] = jnp.concatenate(
        [acc_kv[:head_dim] * head_dim ** (-0.5), acc_kv[head_dim:]], axis=0
    )
    return done


def layer_kernel(
    plan, heads, head_dim,
    att_ref, tok_ref, ob_ref, gain_ref, shift_ref, db_ref, upb_ref, lse_ref, gain_one_ref,
    wo_hbm, cot_hbm, up_hbm, down_hbm, rest_hbm, q_hbm, k_hbm, v_hbm, kt_hbm, normal_hbm, wq_hbm, wkv_hbm,
    sum_ref, out_hbm, end_mat, res_ref,
    gatt_ref, low, inbox, mat, upb_mat, feed_fetch, back_fetch, kv_send, kv_recv, load, *summing,
):
    me = lax.axis_index("seq")
    shard_len, width = tok_ref.shape
    pieces, height, _ = mat.shape
    half = len(summing) // 2
    summed = Summing(plan, pieces, height, mat, *summing[:2], summing[2:half])
    ending = Summing(plan, *end_mat.shape[:2], end_mat, *summing[half : half + 2], summing[half + 2 :])
    starts = summed.starts(DELAYS)
    greet(plan, me, summed.partners())
    for t in range(upb_mat.shape[0]):
        wide_t = upb_mat.shape[2]
        upb_mat[t] = upb_ref[pl.ds(t * wide_t, wide_t)].reshape(1, wide_t)

    def store(p):
        pltpu.make_async_copy(mat.at[p], sum_ref.at[p], load.at[p]).start()

    def talk(n):
        summed.step(n, starts, None, store)

    def first(up_buf, down_buf, normal, out_acc, gn_acc, wo_ref, cot_ref, out_ref):
        feed_phase(
            att_ref, wo_hbm, tok_ref, cot_hbm, (ob_ref, gain_ref, shift_ref, db_ref), upb_mat, up_hbm, down_hbm,
            out_hbm, res_ref, gatt_ref, mat,
            up_buf, down_buf, normal, out_acc, gn_acc, wo_ref, cot_ref, out_ref, feed_fetch, talk,
        )

    tile = height // 2
    pl.run_scoped(
        first,
        pltpu.VMEM((2, width, tile), bf16),
        pltpu.VMEM((2, tile, width), bf16),
        pltpu.VMEM((shard_len, width), bf16),
        pltpu.VMEM((shard_len, width), f32),
        pltpu.VMEM((shard_len, width), f32),
        pltpu.VMEM((width, width), bf16),
        pltpu.VMEM((shard_len, width), bf16),
        pltpu.VMEM((shard_len, width), bf16),
    )
    talk(pieces - 1)
    window, columns = plan.window, heads * CHUNK
    chunks = plan.per_dev

    def second(k_ref, v_ref, kt_ref, q_ref, q_mat, q_aug, g_aug, acc, total, spare, wkv):
        copies = [
            pltpu.make_async_copy(src, dst, back_fetch.at[5 + k])
            for k, (src, dst) in enumerate([(normal_hbm, gatt_ref), (wq_hbm, spare), (wkv_hbm, wkv)])
        ]

        def later():
            for copy in copies:
                copy.start()

        done = back_phase(
            plan, heads, head_dim, me, talk, pieces,
            q_hbm, k_hbm, v_hbm, kt_hbm, lse_ref, att_ref, rest_hbm, gatt_ref, q_ref,
            low, inbox, kv_send, kv_recv,
            k_ref, v_ref, kt_ref, q_ref, q_mat, q_aug, g_aug, acc, total, spare, back_fetch, later,
        )

        for copy in copies:
            copy.wait()
        normal, wq = gatt_ref, spare
        end_height = end_mat.shape[1]
        grad = contract(normal[...], q_ref[...], 0, 1).astype(bf16)
        end_mat[0] = grad[:end_height]
        end_mat[1, : width - end_height, :] = grad[end_height:]
        ending.event(0, 0)
        grad_qb = jnp.sum(q_ref[...].astype(f32).T, axis=0, keepdims=True)
        gn = contract(q_ref[...], wq[...], 0, 1)

        def drain(n, _):
            talk(n)
            return 0

        lax.fori_loop(done, starts[-1] + pieces, drain, 0)
        for off in range(1, plan.reach + 1):

            @pl.when(plan.feeds(me, me + off))
            def _():
                at = pl.ds(pl.multiple_of(plan.place(me, me + off), CHUNK), shard_len)
                remote(
                    low.at[:, at], inbox.at[off - 1], kv_send.at[off - 1], kv_recv.at[off - 1], me + off
                ).wait_recv()
                total[:, :shard_len] += inbox[off - 1].astype(f32)

            @pl.when(plan.feeds(me - off, me))
            def _():
                at = pl.ds(pl.multiple_of(plan.place(me - off, me), CHUNK), shard_len)
                remote(
                    low.at[:, at], inbox.at[off - 1], kv_send.at[off - 1], kv_recv.at[off - 1], me - off
                ).wait_send()

        grad_kv = total[:, :shard_len].astype(bf16)
        gn = gn + contract(grad_kv, wkv[...], 0, 1)
        at = width - end_height
        end_mat[1, at : at + 2 * head_dim, :] = contract(grad_kv, normal[...], 1, 0).astype(bf16)
        grad_vb = jnp.sum(grad_kv.astype(f32).T, axis=0, keepdims=True)

        tok = tok_ref[...].astype(f32)
        center = tok - jnp.mean(tok, axis=-1, keepdims=True)
        scale = lax.rsqrt(jnp.mean(center * center, axis=-1, keepdims=True) + epsilon)
        xhat = center * scale
        grads = [gn * xhat, gn]
        rows = [jnp.sum(grad, axis=0, keepdims=True) for grad in grads] + [grad_qb]
        rows.append(jnp.concatenate([grad_vb, jnp.zeros((1, width - 2 * head_dim), f32)], axis=1))
        rows.append(jnp.zeros((16 - len(rows), width), f32))
        at = at + 2 * head_dim
        end_mat[1, at : at + 16, :] = jnp.concatenate(rows, axis=0).astype(bf16)
        end_mat[1, at + 16 :, :] = jnp.zeros((end_height - at - 16, width), bf16)
        ending.event(0, 1)
        q = gn * line(gain_one_ref)
        res_ref[...] += scale * (
            q - jnp.mean(q, axis=-1, keepdims=True) - xhat * jnp.mean(q * xhat, axis=-1, keepdims=True)
        )

        for stage in range(1, ending.stages + 1):
            for p in range(2):
                ending.event(stage, p)

    pl.run_scoped(
        second,
        pltpu.VMEM((window, 4 * head_dim), bf16),
        pltpu.VMEM((window, 2 * head_dim), bf16),
        pltpu.VMEM((head_dim, window), bf16),
        pltpu.VMEM((width, shard_len), bf16),
        pltpu.VMEM((chunks, head_dim, columns), bf16),
        pltpu.VMEM((chunks, 4 * head_dim, columns), bf16),
        pltpu.VMEM((chunks, 2 * head_dim, columns), bf16),
        pltpu.VMEM((chunks, head_dim, columns), f32),
        pltpu.VMEM((2 * head_dim, window), f32),
        pltpu.VMEM(wq_hbm.shape, bf16),
        pltpu.VMEM(wkv_hbm.shape, bf16),
    )
    for p in range(pieces):
        pltpu.make_async_copy(mat.at[p], sum_ref.at[p], load.at[p]).wait()


def final_kernel(
    head_dim,
    sum_ref, rest_ref, last_ref,
    up_ref, down_ref, out_ref, q_ref, kv_ref, upb_ref,
    db_ref, ob_ref, gain_two_ref, shift_two_ref, gain_one_ref, shift_one_ref, qb_ref, vb_ref,
):
    i = pl.program_id(0)
    tile, width = down_ref.shape
    up_ref[...] = sum_ref[0, :tile, :].astype(f32).T
    down_ref[...] = sum_ref[0, tile:, :].astype(f32)

    @pl.when(i == 0)
    def _():
        out_ref[...] = rest_ref[0, :width, :].astype(f32)
        q_ref[:tile, :] = last_ref[0].astype(f32)
        at = width - tile
        q_ref[tile:, :] = last_ref[1, :at, :].astype(f32)
        kv_ref[...] = last_ref[1, at : at + 2 * head_dim, :].astype(f32).T
        rows = rest_ref[0, width : width + 32, :].astype(f32)
        for k, ref in enumerate([db_ref, ob_ref, gain_two_ref, shift_two_ref]):
            ref[...] = rows[k : k + 1].reshape(width)
        for t in range(upb_ref.shape[0] // tile):
            upb_ref[pl.ds(t * tile, tile)] = rows[16 + t : 17 + t, :tile].reshape(tile)
        at = at + 2 * head_dim
        rows = last_ref[1, at : at + 16, :].astype(f32)
        for k, ref in enumerate([gain_one_ref, shift_one_ref, qb_ref]):
            ref[...] = rows[k : k + 1].reshape(width)
        vb_ref[...] = rows[3:4, head_dim : 2 * head_dim].reshape(head_dim)


def whole(shape):
    return pl.BlockSpec(shape, lambda i: (0,) * len(shape))


def column(height):
    return pl.BlockSpec((height, CHUNK), lambda i: (0, i))


def lead(shape):
    return pl.BlockSpec((1,) + shape, lambda i: (i,) + (0,) * len(shape))


def per_device(
    plan,
    tokens,
    lengths,
    cotangent,
    norm1_gain,
    norm1_shift,
    query_weight,
    query_bias,
    keyval_weight,
    value_bias,
    out_weight,
    out_bias,
    norm2_gain,
    norm2_shift,
    up_weight,
    up_bias,
    down_weight,
    down_bias,
):
    shard_len, width = tokens.shape[1:]
    head_dim = keyval_weight.shape[1] // 2
    heads = width // head_dim
    columns = heads * CHUNK
    chunks = plan.per_dev
    window = plan.window
    reach = plan.reach
    limit = dict(vmem_limit_bytes=63 * 2**20)
    vmem = pl.BlockSpec(memory_space=pltpu.VMEM)
    anywhere = pl.BlockSpec(memory_space=pl.ANY)
    dma = pltpu.SemaphoreType.DMA

    normal_one, queries, keyvals = pl.pallas_call(
        partial(gather_kernel, plan),
        in_specs=[vmem] * 7,
        out_specs=[vmem] * 3,
        out_shape=[
            jax.ShapeDtypeStruct((shard_len, width), bf16),
            jax.ShapeDtypeStruct((width, shard_len), bf16),
            jax.ShapeDtypeStruct((window, 2 * head_dim), bf16),
        ],
        scratch_shapes=[pltpu.VMEM((shard_len, 2 * head_dim), bf16)] + [dma((reach,))] * 2,
        compiler_params=pltpu.CompilerParams(collective_id=0, has_side_effects=True, **limit),
        name="gather",
    )(
        tokens[0],
        norm1_gain,
        norm1_shift,
        keyval_weight,
        value_bias,
        query_weight,
        query_bias,
    )

    attended, attended_low, lse, k_aug, v_aug, k_turned = pl.pallas_call(
        partial(attend_kernel, plan, heads, head_dim),
        grid_spec=pltpu.PrefetchScalarGridSpec(
            num_scalar_prefetch=0,
            grid=(chunks,),
            in_specs=[
                pl.BlockSpec(memory_space=pltpu.SMEM),
                column(width),
                whole((window, 2 * head_dim)),
            ],
            out_specs=[
                column(width),
                column(width),
                lead((1, columns)),
                whole((window, 4 * head_dim)),
                whole((window, 2 * head_dim)),
                whole((head_dim, window)),
            ],
            scratch_shapes=[
                pltpu.VMEM((head_dim + 16, window), bf16),
                pltpu.VMEM((head_dim + 16, columns), f32),
                pltpu.VMEM((1, columns), f32),
                pltpu.VMEM((1, 1), f32),
            ],
        ),
        out_shape=[
            jax.ShapeDtypeStruct((width, shard_len), bf16),
            jax.ShapeDtypeStruct((width, shard_len), bf16),
            jax.ShapeDtypeStruct((chunks, 1, columns), f32),
            jax.ShapeDtypeStruct((window, 4 * head_dim), bf16),
            jax.ShapeDtypeStruct((window, 2 * head_dim), bf16),
            jax.ShapeDtypeStruct((head_dim, window), bf16),
        ],
        compiler_params=pltpu.CompilerParams(**limit),
        name="attend",
    )(lengths, queries, keyvals)

    inputs = tokens[0].astype(f32)
    hidden = up_weight.shape[1]
    tile = PIECE // 2
    tiles = hidden // tile
    pieces = tiles + 1
    sums, outputs, last, grad_inputs = pl.pallas_call(
        partial(layer_kernel, plan, heads, head_dim),
        in_specs=[vmem] * 9 + [anywhere] * 12,
        out_specs=[anywhere] * 2 + [vmem] * 2,
        out_shape=[
            jax.ShapeDtypeStruct((pieces, PIECE, width), bf16),
            jax.ShapeDtypeStruct((shard_len, width), bf16),
            jax.ShapeDtypeStruct((2, tile, width), bf16),
            jax.ShapeDtypeStruct((shard_len, width), f32),
        ],
        scratch_shapes=[
            pltpu.VMEM((width, shard_len), bf16),
            pltpu.VMEM((2 * head_dim, window), bf16),
            pltpu.VMEM((reach, 2 * head_dim, shard_len), bf16),
            pltpu.VMEM((pieces, PIECE, width), bf16),
            pltpu.VMEM((tiles, 1, tile), f32),
            dma((3, 2)),
            dma((8,)),
            dma((reach,)),
            dma((reach,)),
            dma((pieces,)),
        ]
        + Summing.scratch(plan, pieces, PIECE, width)
        + Summing.scratch(plan, 2, tile, width),
        compiler_params=pltpu.CompilerParams(collective_id=1, has_side_effects=True, **limit),
        name="layer",
    )(
        attended,
        tokens[0],
        out_bias,
        norm2_gain,
        norm2_shift,
        down_bias,
        up_bias,
        lse,
        norm1_gain,
        out_weight,
        cotangent[0],
        up_weight,
        down_weight,
        attended_low,
        queries,
        k_aug,
        v_aug,
        k_turned,
        normal_one,
        query_weight,
        keyval_weight,
    )

    vector = jax.ShapeDtypeStruct((width,), f32)
    finals = pl.pallas_call(
        partial(final_kernel, head_dim),
        grid=(tiles,),
        in_specs=[
            lead((PIECE, width)),
            pl.BlockSpec((1, PIECE, width), lambda i: (tiles, 0, 0)),
            whole((2, tile, width)),
        ],
        out_specs=[
            pl.BlockSpec((width, tile), lambda i: (0, i)),
            pl.BlockSpec((tile, width), lambda i: (i, 0)),
            whole((width, width)),
            whole((width, width)),
            whole((width, 2 * head_dim)),
            whole((hidden,)),
        ]
        + [whole((width,))] * 7
        + [whole((head_dim,))],
        out_shape=[
            jax.ShapeDtypeStruct((width, hidden), f32),
            jax.ShapeDtypeStruct((hidden, width), f32),
            jax.ShapeDtypeStruct((width, width), f32),
            jax.ShapeDtypeStruct((width, width), f32),
            jax.ShapeDtypeStruct((width, 2 * head_dim), f32),
            jax.ShapeDtypeStruct((hidden,), f32),
        ]
        + [vector] * 7
        + [jax.ShapeDtypeStruct((head_dim,), f32)],
        compiler_params=pltpu.CompilerParams(**limit),
        name="finals",
    )(sums, sums, last)
    up_w, down_w, out_w, qw, kvw, up_b = finals[:6]
    down_b, out_b, gain_two, shift_two, gain_one, shift_one, qb, vb = finals[6:]
    return (
        outputs[None],
        grad_inputs[None],
        gain_one,
        shift_one,
        qw,
        qb,
        kvw,
        vb,
        out_w,
        out_b,
        gain_two,
        shift_two,
        up_w,
        up_b,
        down_w,
        down_b,
    )


def solution(mesh):
    split = P("dp", "seq", None)
    devices = mesh.shape["seq"]

    def run(*arrays):
        plan = Plan(devices, arrays[0].shape[1] // devices)
        return jax.shard_map(
            partial(per_device, plan),
            mesh=mesh,
            in_specs=(split, P("dp", None), split) + (P(),) * 14,
            out_specs=(split, split) + (P(),) * 14,
            check_vma=False,
        )(*arrays)

    return run
```

time: 1550 us -> 310 us (0.20)
  matrix products: 740 us -> 0 us
  waiting for transfers between devices: 330 us -> 0 us
  Pallas kernels: 0 us -> 305 us
  other arithmetic: 295 us -> 0 us
  blocking collectives: 76 us -> 0 us
  local copies, waits for them, and re-layouts: 50.4 us -> 3.92 us
  starting transfers between devices: 30 us -> 0 us
    dot_general x57 -> x0, matrix products: 740 us -> none  [the longest x12 171 us: scores_of(): jnp.einsum('qhd,kd->hqk', query_pair, key_part, preferred_element_type=jn...]
    psum x1 -> x0, waiting for transfers between devices: 313 us -> none  [per_device(): lax.psum((grad_gain_one, grad_shift_one, grad_qw, grad_qb, grad_kvw, grad...]
    pallas_call x0 -> x4, Pallas kernels: none -> 305 us  [the longest x1 257 us: per_device(): pl.pallas_call(partial(layer_kernel, plan, heads, head_dim), in_specs=[vm...]
    convert_element_type x8 -> x0, other arithmetic: 173 us -> none  [the longest x6 172 us: backward_pair(): grad_scores = (probability * centered).astype(jnp.bfloat16)]
    reduce_sum x17 -> x0, other arithmetic: 108 us -> none  [the longest x6 98 us: forward_pair(): row_total = jnp.sum(exponent, axis=-1, keepdims=True)]
    psum x1 -> x0, blocking collectives: 76 us -> none  [per_device(): lax.psum((grad_gain_one, grad_shift_one, grad_qw, grad_qb, grad_kvw, grad...]
    unnamed x167 -> x4, local copies, waits for them, and re-layouts: 38.8 us -> 3.92 us
    ppermute x12 -> x0, starting transfers between devices: 30 us -> none  [shifted(): return lax.ppermute(value, axis, pairs)]
  transfers between devices with their start and end apart: 13 -> 0, of which waited for: 3 -> 0; matrix products, arithmetic and copies ran while one was open for 4% -> 0% of each run, Pallas kernels for 0% -> 0%
where the time goes in v2:
time: 310 us; the launch traced here: 309 us
  Pallas kernels  305 us (98%)
  local copies, waits for them, and re-layouts  3.92 us (1%)
    pallas_call x1, Pallas kernels, per_device(): pl.pallas_call(partial(layer_kernel, plan, heads, head_dim), in_specs=[vm...  257 us
    pallas_call x1, Pallas kernels, per_device(): pl.pallas_call(partial(gather_kernel, plan), in_specs=[vmem] * 7, out_spe...  17.3 us
    pallas_call x1, Pallas kernels, per_device(): pl.pallas_call(partial(attend_kernel, plan, heads, head_dim), grid_spec=p...  15.8 us
    pallas_call x1, Pallas kernels, per_device(): pl.pallas_call(partial(final_kernel, head_dim), grid=(tiles,), in_specs=[...  14.4 us

profile of v2, /device:TPU:0, one launch (start us, length us, event | category | flops | bytes accessed | tf_op | source)
XLA Modules:
  0.0 309.1 jit_solution(13154252292255184792)
XLA Ops:
  0.6 17.3 %gather.1 = (bf16[768,768]{1,0:T(8,128)(2,1)}, bf16[768,768]{1,0:T(8,128)(2,1)}, bf16[5120,128]{1,0:T(8,128)(2,1)}) custom-call(bf16[768,768]{1,0:T(8,128)(2,1)} %bitcast.4, f32[768]{0:T(1024)} %gain_one_ref.1, f32[768]{0:T(1024)} %shift_ref.2, bf16[768,128]{1,0:T(8,128)(2,1)} %wkv_hbm.1, f32[64]{0:T(128)} %kvb_ref.1, bf16[768,768]{1,0:T(8,128)(2,1)} %wq_hbm.1, ...), custom_call_target="tpu_custom_call" | custom-call | tf_op jit(solution)/shard_map/gather/pallas_call | solution.py:816
  18.0 15.8 %attend.1 = (bf16[768,768]{1,0:T(8,128)(2,1)}, bf16[768,768]{1,0:T(8,128)(2,1)}, f32[6,1,1536]{2,1,0:T(1,128)}, bf16[5120,256]{1,0:T(8,128)(2,1)}, bf16[5120,128]{1,0:T(8,128)(2,1)}, /*index=5*/bf16[64,5120]{1,0:T(8,128)(2,1)}) custom-call(s32[1,3]{1,0:T(1,128)} %len_ref.1, bf16[768,768]{1,0:T(8,128)(2,1)} %get-tuple-element.43.q_ref.q_hbm, ...), custom_call_target="tpu_custom_call" | custom-call | tf_op jit(solution)/shard_map/attend/pallas_call | solution.py:838
  33.7 257.0 %layer.1 = (bf16[7,1024,768]{2,1,0:T(8,128)(2,1)}, bf16[768,768]{1,0:T(8,128)(2,1)}, bf16[2,512,768]{2,1,0:T(8,128)(2,1)}, f32[768,768]{1,0:T(8,128)}) custom-call(bf16[768,768]{1,0:T(8,128)(2,1)} %get-tuple-element.45.att_ref, bf16[768,768]{1,0:T(8,128)(2,1)} %bitcast.5, f32[768]{0:T(1024)} %ob_ref.1, f32[768]{0:T(1024)} %gain_ref.3, f32[768]{0:T(1024)} %shift_ref.3, ...), custom_call_target="tpu_custom_call" | custom-call | tf_op jit(solution)/shard_map/layer/pallas_call | solution.py:880
  290.8 14.4 %finals.1 = (f32[768,3072]{1,0:T(8,128)}, f32[3072,768]{1,0:T(8,128)}, f32[768,768]{1,0:T(8,128)}, f32[768,768]{1,0:T(8,128)}, f32[768,128]{1,0:T(8,128)}, /*ind...) custom-call(bf16[7,1024,768]{2,1,0:T(8,128)(2,1)} %get-tuple-element, ...), custom_call_target="tpu_custom_call" | custom-call | tf_op jit(solution)/shard_map/finals/pallas_call | solution.py:931
  305.2 0.0 copy-start
  305.2 2.5 copy.35
  307.7 0.0 copy-done
  307.7 1.4 copy.36
Async XLA Ops:
  305.2 2.5 copy-start
